TPU v7x, 32 devices: a whole 2x2x4 slice. The times are simulated.
32 devices in a mesh: copy: 4 (over x, core), space: 8 (over z, y).
Axes of the slice: x: 2, y: 2, z: 4, core: 2. Of those that a mesh axis runs over, the one named last changes fastest.
Arguments:
- noisy_tokens: bfloat16 [4, 256, 256, 384], P('copy', 'space'), may hold values from -6 to 6
- grad_out: bfloat16 [4, 256, 256, 384], P('copy', 'space'), may hold values from -6 to 6
- filter_weight: bfloat16 [2, 256, 256, 384], P(None, None, 'space'), may hold values from -4 to 4
- weight_in: bfloat16 [384, 1536], replicated, may hold values from -0.3125 to 0.3125
- weight_out: bfloat16 [1536, 384], replicated, may hold values from -0.15625 to 0.15625
- gain_one: float32 [384], replicated, may hold values from 0.1 to 1.9
- gain_two: float32 [384], replicated, may hold values from 0.1 to 1.9
Outputs:
- block_out: bfloat16 [4, 256, 256, 384], P('copy', 'space')
- grad_tokens: bfloat16 [4, 256, 256, 384], P('copy', 'space')
- grad_filter: float32 [2, 256, 256, 384], P(None, None, 'space')
- grad_weight_in: bfloat16 [384, 1536], replicated
- grad_weight_out: bfloat16 [1536, 384], replicated
- grad_gain_one: float32 [384], replicated
- grad_gain_two: float32 [384], replicated
All inputs are finite; a program needn't handle non-finite values.
Results may differ from a plain program's by a relative error of at most 0.024.
Values may be sent and summed in bfloat16 or wider, within the bound.
No kernel may reach another device: no remote copies, remote signals or barrier semaphores. Data moves between devices by JAX's collectives and lax.ppermute only.
A program may use at most 320 MiB of HBM per device.

v0:
```python
import functools
import math

import jax
import jax.numpy as jnp
import ml_dtypes
import numpy as np
from jax import lax
from jax.experimental import pallas as pl
from jax.experimental.pallas import tpu as pltpu
from jax.sharding import PartitionSpec as P

EPS = 1e-06
LANES = 128
VMEM_LIMIT = 60 * 1024 * 1024
BF16 = jnp.bfloat16
F32 = jnp.float32


def dft_pair(length):
    index = np.arange(length, dtype=np.int64)
    angle = (index[:, None] * index[None, :] % length) * (2.0 * math.pi / length)
    factor = 1.0 / math.sqrt(length)
    rounded = lambda a: a.astype(np.float32).astype(ml_dtypes.bfloat16).astype(np.float32)
    return rounded(np.cos(angle) * factor), rounded(np.sin(angle) * factor)


def row_tables(width, n):
    cosine, sine = dft_pair(width)
    own = width // n
    half = own // 2
    forward = np.zeros((n, 2, half, width), np.float32)
    weight = np.full((n, 2, half, 1), 2.0, np.float32)
    for d in range(n):
        first = own * d + (1 if d >= n // 2 else 0)
        forward[d, 0] = cosine[first : first + half]
        forward[d, 1] = -sine[first : first + half]
    forward[0, 1, 0] = cosine[width // 2]
    weight[0, :, 0] = 1.0
    shape = (n, 2 * half, width)
    return (
        forward.reshape(shape).astype(ml_dtypes.bfloat16),
        (forward * weight).reshape(shape).astype(ml_dtypes.bfloat16),
    )


def column_tables(height, n, chunks):
    cosine, sine = dft_pair(height)
    zero = np.zeros_like(cosine)
    rows = height // n // chunks

    def arrange(blocks):
        full = np.stack([np.stack(line, axis=1) for line in blocks])
        full = full.reshape(2 * height, 2, n, chunks, rows)
        return full.transpose(0, 3, 2, 1, 4).reshape(2 * height, 2 * height)

    middle = arrange([[zero, cosine], [zero, -sine]])
    first = arrange([[cosine, zero], [-sine, zero]])
    other = arrange([[cosine, sine], [-sine, cosine]])
    backward = np.stack([middle, first, other]).transpose(0, 2, 1)
    backward = backward.reshape(3, chunks, n, 2 * rows, 2 * height)
    return backward.astype(ml_dtypes.bfloat16)


def mirror_table(height):
    table = np.zeros((height, height), np.float32)
    table[np.arange(height), (-np.arange(height)) % height] = 1.0
    return table.astype(ml_dtypes.bfloat16)


def dot(a, b):
    return jnp.dot(a, b, preferred_element_type=F32)


def dot_tn(a, b):
    return lax.dot_general(a, b, (((0,), (0,)), ((), ())), preferred_element_type=F32)


def normalize(values):
    centred = values - jnp.mean(values, axis=-1, keepdims=True)
    variance = jnp.mean(centred * centred, axis=-1, keepdims=True)
    rstd = lax.rsqrt(variance + EPS)
    return centred * rstd, rstd


def norm_backward(upstream, normed, rstd, gain):
    scaled = upstream * gain
    return (
        scaled
        - jnp.mean(scaled, axis=-1, keepdims=True)
        - normed * jnp.mean(scaled * normed, axis=-1, keepdims=True)
    ) * rstd


def gelu_and_slope(v):
    e = jnp.exp(v * v * -0.5)
    d = 1.0 + (0.3275911 / math.sqrt(2.0)) * jnp.abs(v)
    t = pl.reciprocal(d, approx=True)
    t = t * (2.0 - d * t)
    poly = 0.5 * 1.061405429
    for coefficient in (-1.453152027, 1.421413741, -0.284496736, 0.254829592):
        poly = poly * t + 0.5 * coefficient
    tail = poly * t * e
    phi = jnp.where(v < 0.0, tail, 1.0 - tail)
    return v * phi, phi + v * e * (1.0 / math.sqrt(2.0 * math.pi))


def spaced(count):
    groups = -(-count // 8)
    return 8 * (groups + 1 - groups % 2)


def lanes(c):
    return slice(c * LANES, (c + 1) * LANES)


def unpack(received, scratch):
    count, rows, chans = received[0].shape
    pitch = spaced(rows)

    def step(k, carry):
        for s, ref in enumerate(received):
            start = pl.multiple_of((s * count + k) * pitch, 8)
            for c in range(chans // LANES):
                scratch[c, pl.ds(start, rows), :] = ref[k, :, lanes(c)].astype(F32)
        return carry

    lax.fori_loop(0, count, step, 0, unroll=2)


def read_row(scratch, row, columns, rows):
    parts = [
        scratch[c, pl.ds(row, columns, stride=spaced(rows)), :].astype(BF16)
        for c in range(scratch.shape[0])
    ]
    return jnp.concatenate(parts, axis=1)


def write_row(scratch, row, columns, values):
    start = pl.multiple_of(row * spaced(columns), 8)
    for c in range(scratch.shape[0]):
        scratch[c, pl.ds(start, columns), :] = values[:, lanes(c)]


def pack(scratch, columns, outgoing):
    count, rows, _ = outgoing[0].shape

    def step(k, carry):
        for s, ref in enumerate(outgoing):
            for c in range(scratch.shape[0]):
                part = scratch[c, pl.ds(s * count + k, rows, stride=spaced(columns)), :]
                ref[k, :, lanes(c)] = part.astype(BF16)
        return carry

    lax.fori_loop(0, count, step, 0, unroll=2)


def params():
    return pltpu.CompilerParams(vmem_limit_bytes=VMEM_LIMIT)


def resident(shape):
    return pl.BlockSpec(shape, lambda *_: (0,) * len(shape), pipeline_mode=pl.Buffered(1))


ANYWHERE = pl.BlockSpec(memory_space=pl.ANY)


def cost(flops, size):
    return pl.CostEstimate(flops=int(flops), bytes_accessed=int(size), transcendentals=0)


def shape_of(shape, dtype=BF16):
    return jax.ShapeDtypeStruct(tuple(shape), dtype)


def hold(value, after):
    return pl.pallas_call(
        lambda *refs: None,
        in_specs=[ANYWHERE] * (1 + len(after)),
        out_specs=ANYWHERE,
        out_shape=shape_of(value.shape, value.dtype),
        input_output_aliases={0: 0},
        compiler_params=params(),
        cost_estimate=cost(0, 0),
        name="hold",
    )(value, *after)


def enter_kernel(tokens, gain, table, *rest):
    outgoing, scratch = rest[-2:-1], rest[-1]
    step = pl.program_id(0)
    block, width, _ = tokens.shape
    for r in range(block):
        normed, _ = normalize(tokens[r].astype(F32))
        mixed = (normed * gain[...]).astype(BF16)
        write_row(scratch, step * block + r, width, dot(table[...], mixed))

    @pl.when(step == pl.num_programs(0) - 1)
    def _():
        pack(scratch, width, outgoing)


def enter(tokens, gain, table, block):
    rows, width, chans = tokens.shape
    steps = rows // block
    out = (width, rows, chans)
    return pl.pallas_call(
        enter_kernel,
        grid=(steps,),
        in_specs=[
            pl.BlockSpec((block, width, chans), lambda i: (i, 0, 0)),
            resident((1, chans)),
            resident((width, width)),
        ],
        out_specs=resident(out),
        out_shape=shape_of(out),
        scratch_shapes=[pltpu.VMEM((chans // LANES, rows * spaced(width), LANES), F32)],
        compiler_params=params(),
        cost_estimate=cost(2 * rows * width * width * chans, 4 * rows * width * chans),
        name="enter_rows",
    )(tokens, gain, table)


def mlp_kernel(
    n, later, tokens, upstream, gain, table_out, table_in, w_in, w_out, w_in_t, w_out_t, *rest
):
    received, rest = rest[:n], rest[n:]
    if later:
        (_, *before), rest = rest[:4], rest[4:]
    block_out, outgoing, rest = rest[0], rest[1 : n + 1], rest[n + 1 :]
    sum_in, sum_out, sum_gain, unpacked, packed = rest
    step = pl.program_id(0)
    block, width, chans = tokens.shape
    rows = received[0].shape[1]
    hidden = w_in.shape[1]
    part = min(512, hidden)

    @pl.when(step == 0)
    def _():
        unpack(received, unpacked)
        for i, ref in enumerate((sum_in, sum_out, sum_gain)):
            ref[...] = before[i][...] if later else jnp.zeros_like(ref)

    spatial = jnp.concatenate(
        [
            dot(table_out[...], read_row(unpacked, step * block + r, width, rows))
            for r in range(block)
        ],
        axis=0,
    )
    normed, rstd = normalize(spatial)
    mlp_in = (normed * gain[...]).astype(BF16)
    grad = upstream[...].reshape(block * width, chans)
    out = tokens[...].reshape(block * width, chans).astype(F32)
    grad_mlp = jnp.zeros_like(spatial)

    def first(cols):
        return dot(mlp_in, w_in[:, cols]), dot(grad, w_out_t[:, cols])

    parts = [slice(f, f + part) for f in range(0, hidden, part)]
    ahead = first(parts[0])
    for f, cols in enumerate(parts):
        preact, grad_act = ahead
        if f + 1 < len(parts):
            ahead = first(parts[f + 1])
        value, slope = gelu_and_slope(preact)
        activated = value.astype(BF16)
        grad_pre = (grad_act * slope).astype(BF16)
        out = out + dot(activated, w_out[cols, :])
        grad_mlp = grad_mlp + dot(grad_pre, w_in_t[cols, :])
        sum_out[:, cols] += dot_tn(grad, activated)
        sum_in[:, cols] += dot_tn(mlp_in, grad_pre)
    block_out[...] = out.astype(BF16).reshape(block, width, chans)
    grad_spatial = norm_backward(grad_mlp, normed, rstd, gain[...])
    sum_gain[0:8] += jnp.sum((grad_mlp * normed).reshape(-1, 8, chans), axis=0)
    sum_gain[8:16] += jnp.sum((grad_spatial * spatial).reshape(-1, 8, chans), axis=0)
    sent = grad_spatial.astype(BF16)
    for r in range(block):
        values = dot(table_in[...], sent[r * width : (r + 1) * width])
        write_row(packed, step * block + r, width, values)

    @pl.when(step == pl.num_programs(0) - 1)
    def _():
        pack(packed, width, outgoing)


def mlp(received, tokens, upstream, gain, tables, weights, previous, chunk, block):
    n = len(received)
    count, rows, chans = received[0].shape
    width = tokens.shape[1]
    hidden = weights[0].shape[1]
    steps = rows // block
    by_rows = pl.BlockSpec((block, width, chans), lambda i: (i + chunk * steps, 0, 0))
    operands = [tokens, upstream, gain, *tables, *weights, *received]
    in_specs = [
        by_rows,
        by_rows,
        resident((1, chans)),
        resident((width, width)),
        resident((width, width)),
        resident((chans, hidden)),
        resident((hidden, chans)),
        resident((hidden, chans)),
        resident((chans, hidden)),
    ] + [resident((count, rows, chans))] * n
    aliases = {}
    if previous is not None:
        aliases = {len(operands): 0}
        operands += previous
        in_specs += [ANYWHERE] + [resident(p.shape) for p in previous[1:]]
    flops = 2 * rows * width * chans * (6 * hidden + 2 * width)
    outputs = pl.pallas_call(
        functools.partial(mlp_kernel, n, previous is not None),
        grid=(steps,),
        in_specs=in_specs,
        out_specs=[by_rows]
        + [resident((count, rows, chans))] * n
        + [resident((chans, hidden)), resident((chans, hidden)), resident((16, chans))],
        out_shape=[shape_of(tokens.shape)]
        + [shape_of((count, rows, chans))] * n
        + [shape_of((chans, hidden), F32)] * 2
        + [shape_of((16, chans), F32)],
        scratch_shapes=[
            pltpu.VMEM((chans // LANES, width * spaced(rows), LANES), F32),
            pltpu.VMEM((chans // LANES, rows * spaced(width), LANES), F32),
        ],
        input_output_aliases=aliases,
        compiler_params=params(),
        cost_estimate=cost(flops, 10 * rows * width * chans),
        name="mlp_rows",
    )(*operands)
    return outputs[0], outputs[1 : n + 1], outputs[n + 1 :]


def leave_kernel(n, tokens, upstream, gain, table_out, *rest):
    received, (grad_tokens, unpacked) = rest[:n], rest[-2:]
    step = pl.program_id(0)
    block, width, _ = tokens.shape
    rows = received[0].shape[1]

    @pl.when(step == 0)
    def _():
        unpack(received, unpacked)

    for r in range(block):
        back = dot(table_out[...], read_row(unpacked, step * block + r, width, rows))
        normed, rstd = normalize(tokens[r].astype(F32))
        grad = norm_backward(back, normed, rstd, gain[...])
        grad_tokens[r] = (upstream[r].astype(F32) + grad).astype(BF16)


def leave(received, tokens, upstream, gain, table_out, previous, chunk, block, after):
    n = len(received)
    count, rows, chans = received[0].shape
    width = tokens.shape[1]
    steps = rows // block
    by_rows = pl.BlockSpec((block, width, chans), lambda i: (i + chunk * steps, 0, 0))
    operands = [tokens, upstream, gain, table_out, *received]
    in_specs = [by_rows, by_rows, resident((1, chans)), resident((width, width))]
    in_specs += [resident((count, rows, chans))] * n
    aliases = {}
    if previous is not None:
        aliases = {len(operands): 0}
        operands.append(previous)
        in_specs.append(ANYWHERE)
    operands += after
    in_specs += [ANYWHERE] * len(after)
    return pl.pallas_call(
        functools.partial(leave_kernel, n),
        grid=(steps,),
        in_specs=in_specs,
        out_specs=by_rows,
        out_shape=shape_of(tokens.shape),
        scratch_shapes=[pltpu.VMEM((chans // LANES, width * spaced(rows), LANES), F32)],
        input_output_aliases=aliases,
        compiler_params=params(),
        cost_estimate=cost(2 * rows * width * width * chans, 8 * rows * width * chans),
        name="leave_rows",
    )(*operands)


def columns_kernel(count, outs, back, flags, table_f, table_b, kernel, *rest):
    spectrum, rest = (rest[0], rest[1:]) if back else (None, rest)
    received, (*outgoing, held) = rest[:count], rest[-outs - 1 :]
    step, last = pl.program_id(0), pl.num_programs(0) - 1
    per, _, height, chans = kernel.shape

    def load(j):
        return jnp.concatenate([ref[:, :, j].reshape(-1, chans) for ref in received], axis=0)

    def store(j, values):
        values = values.astype(BF16)
        size = values.shape[0] // len(outgoing)
        for i, ref in enumerate(outgoing):
            n, _, _, rows, _ = ref.shape
            ref[:, :, j] = values[i * size : (i + 1) * size].reshape(n, 2, rows, chans)

    def filtered(slot, found):
        found = found.astype(BF16)
        real, imag = found[:height].astype(F32), found[height:].astype(F32)
        k_real, k_imag = kernel[slot, 0].astype(F32), kernel[slot, 1].astype(F32)
        if back:
            s_real, s_imag = spectrum[slot, 0].astype(F32), spectrum[slot, 1].astype(F32)
            held[slot, 0] = (real * s_real + imag * s_imag).astype(BF16)
            held[slot, 1] = (imag * s_real - real * s_imag).astype(BF16)
            k_imag = -k_imag
        else:
            held[slot, 0] = found[:height]
            held[slot, 1] = found[height:]
        upper = (k_real * real - k_imag * imag).astype(BF16)
        lower = (k_real * imag + k_imag * real).astype(BF16)
        return jnp.concatenate([upper, lower], axis=0)

    @pl.when(step < last)
    def _():
        at = [1 + step * per + i for i in range(per)]
        found = dot(table_f[2], jnp.concatenate([load(j) for j in at], axis=1))
        weighted = [filtered(i, found[:, i * chans : (i + 1) * chans]) for i in range(per)]
        result = dot(table_b[2], jnp.concatenate(weighted, axis=1))
        for i, j in enumerate(at):
            store(j, result[:, i * chans : (i + 1) * chans])

    @pl.when(step == last)
    def _():
        values = load(0)
        kind = 2 - flags[1]
        zero = filtered(0, dot(table_f[kind], values))
        middle = filtered(1, dot(table_f[0], values))
        store(0, dot(table_b[kind], zero) + dot(table_b[0], middle))
        for i in range(2, per):
            held[i] = jnp.zeros_like(held[i])


def columns(flags, tables, kernel, received, outs, spectrum=None, after=()):
    count = len(received)
    n, _, half, rows, chans = received[0].shape
    sent = (n, 2, half, count * rows // outs, chans)
    slots, _, height, _ = kernel.shape
    per = columns_per_step(half)
    held = pl.BlockSpec((per, 2, height, chans), lambda t, flags: (t, 0, 0, 0))
    table = resident((3, 2 * height, 2 * height))
    back = spectrum is not None
    outputs = pl.pallas_call(
        functools.partial(columns_kernel, count, outs, back),
        grid_spec=pltpu.PrefetchScalarGridSpec(
            num_scalar_prefetch=1,
            grid=(slots // per,),
            in_specs=[table, table, held]
            + [held] * back
            + [resident(r.shape) for r in received]
            + [ANYWHERE] * len(after),
            out_specs=[resident(sent)] * outs + [held],
        ),
        out_shape=[shape_of(sent)] * outs + [shape_of(kernel.shape)],
        compiler_params=params(),
        cost_estimate=cost(16 * height * height * chans * slots, 20 * height * chans * slots),
        name="filter_columns",
    )(flags, *tables, kernel, *([spectrum] if back else []), *received, *after)
    return outputs[:outs], outputs[outs]


def columns_per_step(half):
    return 3 if (half - 1) % 3 == 0 else 2 if (half - 1) % 2 == 0 else 1


def slot_count(half):
    per = max(2, columns_per_step(half))
    return half - 1 + per


def filter_part_kernel(copies, flags, mirror, own, *rest):
    mains, extras = rest[:copies], rest[copies : 2 * copies]
    kernel, scr_own, scr_main, scr_extra = rest[-4:]
    part = pl.program_id(0)
    upper, first, me = flags[0], flags[1], flags[2]
    _, height, wide, _ = own.shape
    half = wide // 2
    share = height // copies
    pitch_own, pitch = spaced(wide), spaced(half)

    def spread_own(m, carry):
        scr_own[pl.ds(pl.multiple_of(m * pitch_own, 8), wide), :] = own[0, m].astype(F32)
        return carry

    lax.fori_loop(0, height, spread_own, 0, unroll=8)
    for i in range(copies):
        owner = jnp.bitwise_xor(me, i)

        def spread_main(m, carry):
            at = pl.multiple_of((owner * share + m) * pitch, 8)
            scr_main[pl.ds(at, half), :] = mains[i][0, m].astype(F32)
            return carry

        lax.fori_loop(0, share, spread_main, 0, unroll=8)
        at = pl.multiple_of(owner * share, share)
        scr_extra[pl.ds(at, share), :] = extras[i][0].astype(F32)
    sign = jnp.where(part == 0, 0.5, -0.5)
    extra = scr_extra[...]
    middle = 0.5 * extra + sign * dot(mirror[...], extra.astype(BF16))
    kernel[half, 0] = jnp.where(first == 1, middle, 0.0).astype(BF16)
    for i in range(half + 1, kernel.shape[0]):
        kernel[i, 0] = jnp.zeros((height, LANES), BF16)
    for j in range(half):
        mine = scr_own[pl.ds(j + upper, height, stride=pitch_own), :]
        if j == 0:
            other = scr_main[pl.ds(half - 1, height, stride=pitch), :]
            lower = jnp.where(first == 1, mine, extra)
            other = jnp.where(upper == 1, other, lower)
        else:
            other = scr_main[pl.ds(half - j - upper, height, stride=pitch), :]
        turned = dot(mirror[...], other.astype(BF16))
        kernel[(j - 1) % half, 0] = (0.5 * mine + sign * turned).astype(BF16)


def filter_part(flags, mirror, own, mains, extras, after):
    _, height, wide, chans = own.shape
    copies = len(mains)
    half, share = wide // 2, height // copies
    slots = slot_count(half)
    return pl.pallas_call(
        functools.partial(filter_part_kernel, copies),
        grid_spec=pltpu.PrefetchScalarGridSpec(
            num_scalar_prefetch=1,
            grid=(2, chans // LANES),
            in_specs=[
                pl.BlockSpec((height, height), lambda p, c, flags: (0, 0)),
                pl.BlockSpec((1, height, wide, LANES), lambda p, c, flags: (p, 0, 0, c)),
            ]
            + [pl.BlockSpec((1, share, half, LANES), lambda p, c, flags: (p, 0, 0, c))] * copies
            + [pl.BlockSpec((1, share, LANES), lambda p, c, flags: (p, 0, c))] * copies
            + [ANYWHERE] * len(after),
            out_specs=pl.BlockSpec((slots, 1, height, LANES), lambda p, c, flags: (0, p, 0, c)),
            scratch_shapes=[
                pltpu.VMEM((height * spaced(wide), LANES), F32),
                pltpu.VMEM((height * spaced(half), LANES), F32),
                pltpu.VMEM((height, LANES), F32),
            ],
        ),
        out_shape=shape_of((slots, 2, height, chans)),
        compiler_params=params(),
        cost_estimate=cost(4 * height * height * chans * half, 16 * height * half * chans),
        name="filter_part",
    )(flags, mirror, own, *mains, *extras, *after)


def filter_gradient_kernel(copies, flags, mirror, *rest):
    mine, theirs = rest[:copies], rest[copies : 2 * copies]
    out, gathered, turned = rest[-3:]
    part = pl.program_id(0)
    upper, me = flags[0], flags[2]
    _, height, wide, _ = out.shape
    half = wide // 2
    share = height // copies
    pitch = spaced(height)
    for i in range(copies):
        at = pl.multiple_of(jnp.bitwise_xor(me, i) * share, share)
        gathered[0:half, pl.ds(at, share), :] = mine[i][:, 0]
        gathered[half:, pl.ds(at, share), :] = theirs[i][:, 0]
    sign = jnp.where(part == 0, 1.0, -1.0)
    for k in range(wide):
        if k == 0:
            index = jnp.where(upper == 1, 2 * half, half - 1)
        elif k < half:
            index = k - 1 - upper
            index = jnp.where(index < 0, half - 1, index)
        elif k == half:
            index = jnp.where(upper == 1, half - 2, 2 * half - 2)
        else:
            index = wide - 2 - k + upper
            index = half + jnp.where(index < 0, half - 1, index)
        value = gathered[index]
        if 0 < k < half:
            value = value.astype(F32)
        else:
            other = sign * dot(mirror[...], value)
            if k == 0:
                other = jnp.where(upper == 1, other, value.astype(F32))
            elif k == half:
                other = jnp.where(upper == 1, value.astype(F32), other)
            value = other
        turned[pl.ds(k * pitch, height), :] = value

    def step(m, carry):
        out[0, m] = turned[pl.ds(m, wide, stride=pitch), :]
        return carry

    lax.fori_loop(0, height, step, 0, unroll=8)


def filter_gradient(flags, mirror, mine, theirs, height, wide, after):
    _, _, share, chans = mine[0].shape
    copies, half = len(mine), wide // 2
    block = lambda slots: pl.BlockSpec(
        (slots, 1, share, LANES), lambda p, c, flags: (0, p, 0, c)
    )
    return pl.pallas_call(
        functools.partial(filter_gradient_kernel, copies),
        grid_spec=pltpu.PrefetchScalarGridSpec(
            num_scalar_prefetch=1,
            grid=(2, chans // LANES),
            in_specs=[pl.BlockSpec((height, height), lambda p, c, flags: (0, 0))]
            + [block(half)] * copies
            + [block(half + 1)] * copies
            + [ANYWHERE] * len(after),
            out_specs=pl.BlockSpec((1, height, wide, LANES), lambda p, c, flags: (p, 0, 0, c)),
            scratch_shapes=[
                pltpu.VMEM((wide + 1, height, LANES), BF16),
                pltpu.VMEM((wide * spaced(height), LANES), F32),
            ],
        ),
        out_shape=shape_of((2, height, wide, chans), F32),
        compiler_params=params(),
        cost_estimate=cost(2 * height * height * chans * wide, 12 * height * wide * chans),
        name="filter_gradient",
    )(flags, mirror, *mine, *theirs, *after)


def swap(value, axis, size, partner):
    return lax.ppermute(value, axis, [(i, partner(i)) for i in range(size)])


def swap_bits(value, axis, size, bits):
    return swap(value, axis, size, lambda i: i ^ bits)


def exchange(value):
    return lax.all_to_all(value, "space", split_axis=0, concat_axis=0, tiled=True)


def gather_copies(value, copies):
    parts = {0: value}
    bit = copies // 2
    while bit:
        for key in list(parts):
            parts[key ^ bit] = swap_bits(parts[key], "copy", copies, bit)
        bit //= 2
    return [parts[i] for i in range(copies)]


def reduce_shares(value, axes, extra=None):
    places, place = [], 0
    for name in axes:
        digits = lax.axis_size(name).bit_length() - 1
        places += [(name, bit, place + digits - 1 - bit) for bit in range(digits)]
        place += digits
    for name, bit, place in places:
        size, own = lax.axis_size(name), (lax.axis_index(name) >> bit) & 1
        kept = lax.dynamic_index_in_dim(value, own, place, keepdims=True)
        sent = lax.dynamic_index_in_dim(value, 1 - own, place, keepdims=True)
        other = swap_bits(sent, name, size, 1 << bit)
        value = (kept.astype(F32) + other.astype(F32)).astype(value.dtype)
        if extra is not None:
            extra = extra + swap_bits(extra, name, size, 1 << bit)
    return value, extra


def body(noisy_tokens, grad_out, filter_weight, weight_in, weight_out, gain_one, gain_two):
    _, rows_dev, width, chans = noisy_tokens.shape
    height, wide = filter_weight.shape[1:3]
    digits = (2,) * (lax.axis_size("copy").bit_length() - 1)
    hidden = weight_in.shape[1]
    half = wide // 2
    n, copies = lax.axis_size("space"), lax.axis_size("copy")
    chunks = 2
    rows = rows_dev // chunks
    tokens, upstream = noisy_tokens[0], grad_out[0]
    me, copy = lax.axis_index("space"), lax.axis_index("copy")

    share = height // copies
    at = copy * share
    opposite = lambda d: n - 1 - d
    main = lax.dynamic_slice(filter_weight, (0, at, half, 0), (2, share, half, chans))
    main = swap(main, "space", n, opposite)
    to_lower = [(n // 2, 0)] + [(e, n - e) for e in range(n // 2 + 1, n)]
    single = lax.dynamic_slice(filter_weight, (0, at, 0, 0), (2, share, 1, chans))
    single = lax.ppermute(single.reshape(2, share, chans), "space", to_lower)

    forward, weighted = row_tables(width, n)
    table_in = jnp.asarray(forward.reshape(width, width))
    table_out = jnp.asarray(np.ascontiguousarray(weighted.reshape(width, width).T))
    whole, cut = (
        column_tables(height, n, c).reshape(3, 2 * height, 2 * height) for c in (1, chunks)
    )
    forward_in, backward_in = (
        jnp.asarray(np.ascontiguousarray(t.transpose(0, 2, 1))) for t in (whole, cut)
    )
    out_tabs = jnp.asarray(cut)
    mirror = jnp.asarray(mirror_table(height))
    gain_a, gain_b = gain_one.reshape(1, chans), gain_two.reshape(1, chans)
    upper = (me >= n // 2).astype(jnp.int32)
    first = (me == 0).astype(jnp.int32)

    def flags(index):
        return jnp.stack([upper, first, index.astype(jnp.int32)])

    def split(value):
        return value.reshape(n, 2, half, -1, chans)

    def join(value):
        return value.reshape(width, -1, chans)

    entered = hold(enter(tokens, gain_a, table_in, 2), (main, single))
    arrived = [split(exchange(entered))]
    mains, singles = gather_copies(main, copies), gather_copies(single, copies)
    weights = (weight_in, weight_out, weight_in.T, weight_out.T)
    kernel = filter_part(flags(copy), mirror, filter_weight, mains, singles, weights[2:])
    returned, spectrum = columns(flags(copy), (forward_in, out_tabs), kernel, arrived, chunks)

    tables = (table_out, table_in)
    arrived = []
    previous = None
    for c in range(chunks):
        received = exchange(join(returned[c]))
        block_out, sent, sums = mlp(
            [received], tokens, upstream, gain_b, tables, weights, previous, c, 4
        )
        arrived.append(split(exchange(sent[0])))
        previous = [block_out, *sums]

    axes = ("copy", "space")
    sum_in, sum_out, sum_gain = sums
    both = jnp.concatenate([sum_in, sum_out], axis=0).astype(BF16)
    both = both.reshape((2,) * ((copies * n).bit_length() - 1) + (-1, hidden))
    gains = jnp.stack([jnp.sum(sum_gain[8:], axis=0) / gain_one, jnp.sum(sum_gain[:8], axis=0)])
    part, gains = reduce_shares(both, axes, gains)
    factor = 1.0 / math.sqrt(copies * rows_dev * n * width)
    part = (part.reshape(-1, hidden).astype(F32) * factor).astype(BF16)
    gains = gains * factor

    returned, terms = columns(
        flags(copy), (backward_in, out_tabs), kernel, arrived, chunks, spectrum, (part,)
    )
    grads = lax.all_gather(part, axes, tiled=True)
    received = exchange(join(returned[0]))
    grad_tokens = leave([received], tokens, upstream, gain_a, table_out, None, 0, 2, ())

    terms = terms.reshape(terms.shape[:2] + digits + (share, chans))
    terms = jnp.moveaxis(terms, range(2, 2 + len(digits)), range(len(digits)))
    reduced, _ = reduce_shares(terms, ("copy",))
    reduced = reduced.reshape(-1, 2, share, chans)
    mirrored = swap(reduced[:half], "space", n, opposite)
    to_upper = [(0, n // 2)] + [(d, n - d) for d in range(1, n // 2)]
    single = lax.ppermute(
        jnp.where(me == 0, reduced[half], reduced[half - 1]), "space", to_upper
    )
    mine = gather_copies(reduced[:half], copies)
    received = exchange(hold(join(returned[1]), (mirrored, single)))
    theirs = gather_copies(jnp.concatenate([mirrored, single[None]], axis=0), copies)
    grad_filter = filter_gradient(
        flags(copy), mirror, mine, theirs, height, wide, (grad_tokens,)
    )
    grad_tokens = leave(
        [received], tokens, upstream, gain_a, table_out, grad_tokens, 1, 2, (grad_filter,)
    )
    return (
        block_out[None],
        grad_tokens[None],
        grad_filter,
        grads[:chans],
        grads[chans:].T,
        gains[0],
        gains[1],
    )


def dft_parts(length):
    index = jnp.arange(length, dtype=jnp.int32)
    phase = index[:, None] * index[None, :] % length
    angle = phase.astype(jnp.float32) * (2.0 * math.pi / length)
    factor = 1.0 / math.sqrt(length)
    return (
        (jnp.cos(angle) * factor).astype(jnp.bfloat16),
        (jnp.sin(angle) * factor).astype(jnp.bfloat16),
    )


def row_table(length):
    cosine, sine = dft_parts(length)
    return jnp.stack([cosine, -sine])


def column_table(length, direction):
    cosine, sine = dft_parts(length)
    upper = jnp.stack([cosine, direction * sine], axis=1)
    lower = jnp.stack([-direction * sine, cosine], axis=1)
    return jnp.stack([upper, lower])


def plain_layer_norm(values):
    centre = jnp.mean(values, axis=-1, keepdims=True)
    centred = values - centre
    variance = jnp.mean(centred * centred, axis=-1, keepdims=True)
    rstd_value = lax.rsqrt(variance + EPS)
    return (centred * rstd_value, rstd_value)


def plain_norm_backward(upstream, normed, rstd_value, gain):
    scaled = upstream * gain
    result = (
        scaled
        - jnp.mean(scaled, axis=-1, keepdims=True)
        - normed * jnp.mean(scaled * normed, axis=-1, keepdims=True)
    ) * rstd_value
    lead = tuple(range(upstream.ndim - 1))
    return (result, jnp.sum(upstream * normed, axis=lead))


def apply_filter(spectrum, filter_weight, direction):
    real_part = spectrum[0].astype(jnp.float32)
    imag_part = spectrum[1].astype(jnp.float32)
    kernel_real = filter_weight[0].astype(jnp.float32)
    kernel_imag = direction * filter_weight[1].astype(jnp.float32)
    return jnp.stack(
        [
            kernel_real * real_part - kernel_imag * imag_part,
            kernel_real * imag_part + kernel_imag * real_part,
        ]
    )


def exact_gelu(values):
    return jax.nn.gelu(values, approximate=False)


def spectral(values, filter_weight, direction):
    width = values.shape[2]
    rows_tab = row_table(width)
    rows = jnp.einsum(
        "pkw,bhwc->pbhkc", rows_tab, values, preferred_element_type=jnp.float32
    ).astype(jnp.bfloat16)
    columns = lax.all_to_all(rows, "space", split_axis=3, concat_axis=2, tiled=True)
    height = columns.shape[2]
    spectrum = jnp.einsum(
        "qmph,pbhkc->qbmkc", column_table(height, 1), columns, preferred_element_type=jnp.float32
    ).astype(jnp.bfloat16)
    weighted = apply_filter(spectrum, filter_weight[:, None], direction).astype(jnp.bfloat16)
    returned = jnp.einsum(
        "qmph,pbhkc->qbmkc", column_table(height, -1), weighted, preferred_element_type=jnp.float32
    ).astype(jnp.bfloat16)
    back_rows = lax.all_to_all(returned, "space", split_axis=2, concat_axis=3, tiled=True)
    output = jnp.einsum("pkw,pbhkc->bhwc", rows_tab, back_rows, preferred_element_type=jnp.float32)
    return (output, spectrum)


def plain_body(noisy_tokens, grad_out, filter_weight, weight_in, weight_out, gain_one, gain_two):
    batch, rows_dev, width, chans = noisy_tokens.shape
    inputs = noisy_tokens.astype(jnp.float32)
    normed_one, rstd_one = plain_layer_norm(inputs)
    mixed_in = (normed_one * gain_one).astype(jnp.bfloat16)
    spatial, spectrum = spectral(mixed_in, filter_weight, 1)
    normed_two, rstd_two = plain_layer_norm(spatial)
    mlp_in = (normed_two * gain_two).astype(jnp.bfloat16).reshape(-1, chans)
    preact = jnp.dot(mlp_in, weight_in, preferred_element_type=jnp.float32)
    activated = exact_gelu(preact).astype(jnp.bfloat16)
    mlp_out = jnp.dot(activated, weight_out, preferred_element_type=jnp.float32)
    block_out = (inputs + mlp_out.reshape(inputs.shape)).astype(jnp.bfloat16)
    upstream = grad_out.reshape(-1, chans)
    grad_act = jnp.dot(upstream, weight_out.T, preferred_element_type=jnp.float32)
    grad_pre = jax.vjp(exact_gelu, preact)[1](grad_act)[0].astype(jnp.bfloat16)
    sum_out = jnp.dot(activated.T, upstream, preferred_element_type=jnp.float32)
    sum_in = jnp.dot(mlp_in.T, grad_pre, preferred_element_type=jnp.float32)
    grad_mlp = jnp.dot(grad_pre, weight_in.T, preferred_element_type=jnp.float32).reshape(
        inputs.shape
    )
    grad_spatial, sum_gain_two = plain_norm_backward(grad_mlp, normed_two, rstd_two, gain_two)
    back_spatial, adjoint = spectral(grad_spatial.astype(jnp.bfloat16), filter_weight, -1)
    spec_f = spectrum.astype(jnp.float32)
    adj_f = adjoint.astype(jnp.float32)
    filter_terms = jnp.stack(
        [
            jnp.sum(adj_f[0] * spec_f[0] + adj_f[1] * spec_f[1], axis=0),
            jnp.sum(adj_f[1] * spec_f[0] - adj_f[0] * spec_f[1], axis=0),
        ]
    )
    grad_filter = lax.psum(filter_terms.astype(jnp.bfloat16), "copy").astype(jnp.float32)
    grad_normed, sum_gain_one = plain_norm_backward(back_spatial, normed_one, rstd_one, gain_one)
    grad_tokens = (grad_out.astype(jnp.float32) + grad_normed).astype(jnp.bfloat16)
    local_sums = (sum_in, sum_out, sum_gain_one, sum_gain_two)
    summed = lax.psum(
        (local_sums[0], local_sums[1], local_sums[2], local_sums[3]), ("copy", "space")
    )
    total_tokens = batch * lax.axis_size("copy") * rows_dev * lax.axis_size("space") * width
    factor = 1.0 / math.sqrt(total_tokens)
    return (
        block_out,
        grad_tokens,
        grad_filter,
        (summed[0] * factor).astype(jnp.bfloat16),
        (summed[1] * factor).astype(jnp.bfloat16),
        summed[2] * factor,
        summed[3] * factor,
    )


def solution(mesh):
    def program(*arrays):
        rows_dev, wide = arrays[0].shape[1], arrays[2].shape[2]
        n = lax.axis_size("space")
        tiled = rows_dev % 32 == 0 and wide % 32 == 0 and n & (n - 1) == 0
        return (body if tiled else plain_body)(*arrays)

    return jax.shard_map(
        program,
        mesh=mesh,
        in_specs=(
            P("copy", "space", None, None),
            P("copy", "space", None, None),
            P(None, None, "space", None),
            P(),
            P(),
            P(),
            P(),
        ),
        out_specs=(
            P("copy", "space", None, None),
            P("copy", "space", None, None),
            P(None, None, "space", None),
            P(),
            P(),
            P(),
            P(),
        ),
        check_vma=False,
    )
```

profile of v0, /device:TPU:0, one launch (start us, length us, event | category | flops | bytes accessed | tf_op | source)
XLA Modules:
  0.0 890.5 jit_solution(16095931998267719)
XLA Ops:
  7.2 1.6 constant_dynamic-slice_fusion.9
  8.8 6.1 collective-permute-start
  16.1 1.3 collective-permute-start.4
  18.0 19.0 %enter_rows.1.refs_0_ = bf16[256,32,384]{2,1,0:T(8,128)(2,1)} custom-call(bf16[32,256,384]{2,1,0:T(8,128)(2,1)} %bitcast.40, f32[1,384]{1,0:T(1,128)} %reshape.65.gain, bf16[256,256]{1,0:T(8,128)(2,1)} %constant.87.clone.table.table_in), custom_call_target="tpu_custom_call" | custom-call | flops 1610612736 | bytes 12582912 | tf_op jit(solution)/shard_map/enter_rows/pallas_call | solution.py:208
  37.0 49.3 %collective-permute-done.4.rest_4_.refs_2_ = bf16[2,64,384]{2,1,0:T(8,128)(2,1)S(1)} collective-permute-done((bf16[2,64,384]{2,1,0:T(8,128)(2,1)S(1)}, bf16[2,64,384]{2,1,0:T(8,128)(2,1)S(1)}, u32[]{:S(2)}, u32[]{:S(2)}) %collective-permute-start.4) | collective-permute-done | bytes 98336 | tf_op jit(solution)/shard_map/ppermute | solution.py:677
  88.1 4.9 all-to-all-start
  93.0 1.6 collective-permute-start.2
  94.6 34.0 %collective-permute-done.2.rest_2_ = bf16[2,64,16,384]{3,2,1,0:T(8,128)(2,1)S(1)} collective-permute-done((bf16[2,64,16,384]{3,2,1,0:T(8,128)(2,1)S(1)}, bf16[2,64,16,384]{3,2,1,0:T(8,128)(2,1)S(1)}, u32[]{:S(2)}, u32[]{:S(2)}) %collective-permute-start.2) | collective-permute-done | bytes 1572896 | tf_op jit(solution)/shard_map/ppermute | solution.py:620
  128.6 1.6 collective-permute-start.6
  130.1 2.4 copy.27
  132.5 2.4 copy.28
  137.0 15.4 %filter_part.1.kernel = bf16[18,2,256,384]{3,2,1,0:T(8,128)(2,1)} custom-call(s32[3]{0:T(128)} %pad_add_fusion.flags, bf16[256,256]{1,0:T(8,128)(2,1)} %constant.92.clone.mirror, bf16[2,256,32,384]{3,2,1,0:T(8,128)(2,1)} %own.1, bf16[2,64,16,384]{3,2,1,0:T(8,128)(2,1)} %copy-done.2, bf16[2,64,16,384]{3,2,1,0:T(8,128)(2,1)} %collective-permute-done.1.rest_1_, ...), custom_call_target="tpu_custom_call" | custom-call | flops 1610612736 | bytes 25165824 | tf_op jit(solution)/shard_map/filter_part/pallas_call | solution.py:521
  152.4 78.4 %all-to-all-done = bf16[256,32,384]{2,1,0:T(8,128)(2,1)} async-done(((bf16[256,32,384]{2,1,0:T(8,128)(2,1)}), bf16[256,32,384]{2,1,0:T(8,128)(2,1)}, u32[]{:S(2)}, u32[]{:S(2)}) %all-to-all-start) | async-done | bytes 6291488 | tf_op jit(solution)/shard_map/all_to_all | solution.py:628
  230.8 18.1 %filter_columns.2 = (bf16[8,2,16,16,384]{4,3,2,1,0:T(8,128)(2,1)}, bf16[8,2,16,16,384]{4,3,2,1,0:T(8,128)(2,1)}, bf16[18,2,256,384]{3,2,1,0:T(8,128)(2,1)}) custom-call(s32[3]{0:T(128)} %pad_add_fusion.flags, bf16[3,512,512]{2,1,0:T(8,128)(2,1)} %constant.89.clone.table_f, bf16[3,512,512]{2,1,0:T(8,128)(2,1)} %constant.91.clone.table_b, ...), custom_call_target="tpu_custom_call" | custom-call | flops 7247757312 | bytes 35389440 | tf_op jit(solution)/shard_map/filter_columns/pallas_call | solution.py:444
  248.9 74.7 %all_to_all.35.rest_0_ = bf16[256,16,384]{2,1,0:T(8,128)(2,1)} all-to-all(bf16[256,16,384]{2,1,0:T(8,128)(2,1)} %bitcast.62), channel_id=1, replica_groups=mesh['copy'=4,'space'=8] {'space'}, dimensions={0} | all-to-all | bytes 6291456 | tf_op jit(solution)/shard_map/all_to_all | solution.py:628
  323.6 3.8 all-to-all-start.1
  328.0 66.4 %mlp_rows.2 = (bf16[32,256,384]{2,1,0:T(8,128)(2,1)}, bf16[256,16,384]{2,1,0:T(8,128)(2,1)}, f32[384,1536]{1,0:T(8,128)}, f32[384,1536]{1,0:T(8,128)}, f32[16,384]{1,0:T(8,128)}) custom-call(bf16[32,256,384]{2,1,0:T(8,128)(2,1)} %bitcast.41, bf16[32,256,384]{2,1,0:T(8,128)(2,1)} %bitcast.46, f32[1,384]{1,0:T(1,128)} %reshape.63.gain, ...), custom_call_target="tpu_custom_call" | custom-call | flops 30601641984 | bytes 15728640 | tf_op jit(solution)/shard_map/mlp_rows/pallas_call | solution.py:313
  394.4 3.0 all-to-all-done.1.rest_0_
  397.5 1.7 copy-done.4
  399.1 4.5 all-to-all-start.3
  403.6 68.1 %mlp_rows.3 = (bf16[32,256,384]{2,1,0:T(8,128)(2,1)}, bf16[256,16,384]{2,1,0:T(8,128)(2,1)}, f32[384,1536]{1,0:T(8,128)}, f32[384,1536]{1,0:T(8,128)}, f32[16,384]{1,0:T(8,128)}) custom-call(bf16[32,256,384]{2,1,0:T(8,128)(2,1)} %bitcast.42, bf16[32,256,384]{2,1,0:T(8,128)(2,1)} %bitcast.47, ...), custom_call_target="tpu_custom_call", output_to_operand_aliasing={{0}: (10, {})} | custom-call | flops 30601641984 | bytes 15728640 | tf_op jit(solution)/shard_map/mlp_rows/pallas_call | solution.py:313
  471.7 1.9 convert.10
  474.6 5.9 all-to-all-start.4
  480.5 1.6 add_convert_fusion.1
  482.2 1.5 collective-permute-start.9
  483.7 13.9 %collective-permute-done.9 = bf16[1,1,2,2,2,24,1536]{6,5,4,3,2,1,0:T(8,128)(2,1)S(1)} collective-permute-done((bf16[1,1,2,2,2,24,1536]{6,5,4,3,2,1,0:T(8,128)(2,1)S(1)}, bf16[1,1,2,2,2,24,1536]{6,5,4,3,2,1,0:T(8,128)(2,1)S(1)}, u32[]{:S(2)}, u32[]{:S(2)}) %collective-permute-start.9) | collective-permute-done | bytes 589856 | tf_op jit(solution)/shard_map/ppermute | solution.py:620
  497.9 1.8 collective-permute-start.10
  499.7 14.3 %collective-permute-done.10 = bf16[1,1,2,2,1,24,1536]{6,5,4,3,2,1,0:T(8,128)(2,1)S(1)} collective-permute-done((bf16[1,1,2,2,1,24,1536]{6,5,4,3,2,1,0:T(8,128)(2,1)S(1)}, bf16[1,1,2,2,1,24,1536]{6,5,4,3,2,1,0:T(8,128)(2,1)S(1)}, u32[]{:S(2)}, u32[]{:S(2)}) %collective-permute-start.10) | collective-permute-done | bytes 294944 | tf_op jit(solution)/shard_map/ppermute | solution.py:620
  514.8 21.5 %collective-permute-done.11 = bf16[1,1,2,1,1,24,1536]{6,5,4,3,2,1,0:T(8,128)(2,1)S(1)} collective-permute-done((bf16[1,1,2,1,1,24,1536]{6,5,4,3,2,1,0:T(8,128)(2,1)S(1)}, bf16[1,1,2,1,1,24,1536]{6,5,4,3,2,1,0:T(8,128)(2,1)S(1)}, u32[]{:S(2)}, u32[]{:S(2)}) %collective-permute-start.11) | collective-permute-done | bytes 147488 | tf_op jit(solution)/shard_map/ppermute | solution.py:620
  536.4 18.0 %collective-permute-start.12 = (bf16[1,1,1,1,1,24,1536]{6,5,4,3,2,1,0:T(8,128)(2,1)S(1)}, bf16[1,1,1,1,1,24,1536]{6,5,4,3,2,1,0:T(8,128)(2,1)S(1)}, u32[]{:S(2)}, u32[]{:S(2)}) collective-permute-start(bf16[1,1,1,1,1,24,1536]{6,5,4,3,2,1,0:T(8,128)(2,1)S(1)} %constant_dynamic-slice_fusion.3), channel_id=1, source_target_pairs={{0,4},{1,5},{2,6},{3,7},{4,0},{5,1},{6,2},{7,3},{8,12},{9,13},{10,... | collective-permute-start | bytes 221192 | tf_op jit(solution)/shard_map/ppermute | solution.py:620
  554.4 3.1 collective-permute-done.12
  558.2 19.7 %filter_columns.3 = (bf16[8,2,16,16,384]{4,3,2,1,0:T(8,128)(2,1)}, bf16[8,2,16,16,384]{4,3,2,1,0:T(8,128)(2,1)}, bf16[18,2,256,384]{3,2,1,0:T(8,128)(2,1)}) custom-call(s32[3]{0:T(128)} %pad_add_fusion.flags, bf16[3,512,512]{2,1,0:T(8,128)(2,1)} %constant.90.clone.table_f, bf16[3,512,512]{2,1,0:T(8,128)(2,1)} %constant.91.clone.table_b, ...), custom_call_target="tpu_custom_call" | custom-call | flops 7247757312 | bytes 35389440 | tf_op jit(solution)/shard_map/filter_columns/pallas_call | solution.py:444
  577.8 4.1 constant_dynamic-slice_fusion.2
  581.9 2.2 copy.39
  584.1 5.3 all-to-all-start.6
  590.7 3.3 fusion
  594.3 1.5 collective-permute-start.14
  595.8 39.2 %collective-permute-done.14 = bf16[1,1,18,2,64,384]{5,4,3,2,1,0:T(8,128)(2,1)S(1)} collective-permute-done((bf16[1,1,18,2,64,384]{5,4,3,2,1,0:T(8,128)(2,1)S(1)}, bf16[1,1,18,2,64,384]{5,4,3,2,1,0:T(8,128)(2,1)S(1)}, u32[]{:S(2)}, u32[]{:S(2)}) %collective-permute-start.14) | collective-permute-done | bytes 1769504 | tf_op jit(solution)/shard_map/ppermute | solution.py:620
  635.7 1.4 slice_bitcast_fusion.rest_0_
  637.1 3.3 collective-permute-start.15
  640.4 1.6 collective-permute-start.16
  642.0 36.0 %collective-permute-done.16.refs_2_ = bf16[2,64,384]{2,1,0:T(8,128)(2,1)S(1)} collective-permute-done((bf16[2,64,384]{2,1,0:T(8,128)(2,1)S(1)}, bf16[2,64,384]{2,1,0:T(8,128)(2,1)S(1)}, u32[]{:S(2)}, u32[]{:S(2)}) %collective-permute-start.16) | collective-permute-done | bytes 98336 | tf_op jit(solution)/shard_map/ppermute | solution.py:744
  678.0 1.7 collective-permute-done.15.refs_1_
  680.8 14.6 %all-to-all-done.6.rest_0_ = bf16[256,16,384]{2,1,0:T(8,128)(2,1)} async-done(((bf16[256,16,384]{2,1,0:T(8,128)(2,1)}), bf16[256,16,384]{2,1,0:T(8,128)(2,1)}, u32[]{:S(2)}, u32[]{:S(2)}) %all-to-all-start.6) | async-done | bytes 3145760 | tf_op jit(solution)/shard_map/all_to_all | solution.py:628
  695.4 42.0 %all-to-all-start.5 = ((bf16[256,16,384]{2,1,0:T(8,128)(2,1)}), bf16[256,16,384]{2,1,0:T(8,128)(2,1)S(1)}, u32[]{:S(2)}, u32[]{:S(2)}) async-start(bf16[256,16,384]{2,1,0:T(8,128)(2,1)} %hold.3), calls=%async_computation.5 | async-start | bytes 6291456 | tf_op jit(solution)/shard_map/all_to_all | solution.py:628
  738.1 2.8 pad_maximum_fusion.1.rest_4_
  740.9 1.5 collective-permute-start.21
  743.0 38.2 %collective-permute-done.21.rest_6_ = bf16[17,2,64,384]{3,2,1,0:T(8,128)(2,1)} collective-permute-done((bf16[17,2,64,384]{3,2,1,0:T(8,128)(2,1)}, bf16[17,2,64,384]{3,2,1,0:T(8,128)(2,1)}, u32[]{:S(2)}, u32[]{:S(2)}) %collective-permute-start.21) | collective-permute-done | bytes 1671200 | tf_op jit(solution)/shard_map/ppermute | solution.py:620
  781.7 34.1 %collective-permute-done.18.rest_2_ = bf16[16,2,64,384]{3,2,1,0:T(8,128)(2,1)} collective-permute-done((bf16[16,2,64,384]{3,2,1,0:T(8,128)(2,1)}, bf16[16,2,64,384]{3,2,1,0:T(8,128)(2,1)}, u32[]{:S(2)}, u32[]{:S(2)}) %collective-permute-start.18) | collective-permute-done | bytes 1572896 | tf_op jit(solution)/shard_map/ppermute | solution.py:620
  816.4 2.4 collective-permute-done.23
  818.8 1.6 collective-permute-start.24
  820.4 2.2 collective-permute-done.24
  822.5 1.8 collective-permute-start.25
  824.3 1.9 collective-permute-done.25
  826.2 1.7 collective-permute-start.26
  827.9 1.9 collective-permute-done.26
  829.8 2.6 collective-permute-start.27
  832.4 1.9 collective-permute-done.27
  834.9 3.2 slice_bitcast_fusion.1
  838.1 2.6 copy.32
  840.7 11.4 %leave_rows.2.rest_8_.rest_1_ = bf16[32,256,384]{2,1,0:T(8,128)(2,1)} custom-call(bf16[32,256,384]{2,1,0:T(8,128)(2,1)} %bitcast.43, bf16[32,256,384]{2,1,0:T(8,128)(2,1)} %bitcast.48, f32[1,384]{1,0:T(1,128)} %reshape.65.gain, bf16[256,256]{1,0:T(8,128)(2,1)} %constant.88.clone.table_out, bf16[256,16,384]{2,1,0:T(8,128)(2,1)} %all-to-all-done.6.rest_0_), custom_call_target="tpu_custom_call" | custom-call | flops 805306368 | bytes 12582912 | tf_op jit(solution)/shard_map/leave_rows/pallas_call | solution.py:369
  852.1 18.4 %filter_gradient.1.rest_2_ = f32[2,256,32,384]{3,2,1,0:T(8,128)} custom-call(s32[3]{0:T(128)} %pad_add_fusion.flags, bf16[256,256]{1,0:T(8,128)(2,1)} %constant.92.clone.mirror, bf16[16,2,64,384]{3,2,1,0:T(8,128)(2,1)} %slice_bitcast_fusion.rest_0_, bf16[16,2,64,384]{3,2,1,0:T(8,128)(2,1)} %collective-permute-done.17.rest_1_, ...), custom_call_target="tpu_custom_call" | custom-call | flops 1610612736 | bytes 37748736 | tf_op jit(solution)/shard_map/filter_gradient/pallas_call | solution.py:597
  870.4 1.6 copy-done
  872.1 11.4 %leave_rows.3 = bf16[32,256,384]{2,1,0:T(8,128)(2,1)} custom-call(bf16[32,256,384]{2,1,0:T(8,128)(2,1)} %bitcast.44, bf16[32,256,384]{2,1,0:T(8,128)(2,1)} %bitcast.49, f32[1,384]{1,0:T(1,128)} %reshape.65.gain, bf16[256,256]{1,0:T(8,128)(2,1)} %constant.88.clone.table_out, bf16[256,16,384]{2,1,0:T(8,128)(2,1)} %copy-done, ...), custom_call_target="tpu_custom_call", output_to_operand_aliasing={{}: (5, {})} | custom-call | flops 805306368 | bytes 12582912 | tf_op jit(solution)/shard_map/leave_rows/pallas_call | solution.py:369
  (95 shorter events, 15.4 us)
Async XLA Ops:
  7.2 10.3 %copy-start.15 = (f32[384]{0:T(512)S(1)}, f32[384]{0:T(512)}, u32[]{:S(2)}) copy-start(f32[384]{0:T(512)} %param.18) | copy-start | bytes 4612
  8.8 77.5 %collective-permute-start = (bf16[2,64,16,384]{3,2,1,0:T(8,128)(2,1)S(1)}, bf16[2,64,16,384]{3,2,1,0:T(8,128)(2,1)S(1)}, u32[]{:S(2)}, u32[]{:S(2)}) collective-permute-start(bf16[2,64,16,384]{3,2,1,0:T(8,128)(2,1)S(1)} %constant_dynamic-slice_fusion.9), channel_id=1, source_target_pairs={{0,7},{1,6},{2,5},{3,4},{4,3},{5,2},{6,1},{7,0},{8,15},{9,14},{10,... | collective-permute-start | bytes 4718600 | tf_op jit(solution)/shard_map/ppermute | solution.py:620
  16.1 70.2 %collective-permute-start.4 = (bf16[2,64,384]{2,1,0:T(8,128)(2,1)S(1)}, bf16[2,64,384]{2,1,0:T(8,128)(2,1)S(1)}, u32[]{:S(2)}, u32[]{:S(2)}) collective-permute-start(bf16[2,64,384]{2,1,0:T(8,128)(2,1)S(1)} %bitcast.65), channel_id=1, source_target_pairs={{4,0},{5,3},{6,2},{7,1},{12,8},{13,11},{14,10},{15,9},{20,16},{21,... | collective-permute-start | bytes 294920 | tf_op jit(solution)/shard_map/ppermute | solution.py:677
  86.3 0.7 copy-start.9
  87.0 1.1 copy-start.2
  88.1 4.9 copy-start.3
  88.1 40.5 %copy-start.10 = (bf16[2,64,384]{2,1,0:T(8,128)(2,1)S(1)}, bf16[2,64,384]{2,1,0:T(8,128)(2,1)}, u32[]{:S(2)}) copy-start(bf16[2,64,384]{2,1,0:T(8,128)(2,1)} %copy-done.9) | copy-start | bytes 294916
  88.1 142.6 %all-to-all-start = ((bf16[256,32,384]{2,1,0:T(8,128)(2,1)}), bf16[256,32,384]{2,1,0:T(8,128)(2,1)}, u32[]{:S(2)}, u32[]{:S(2)}) async-start(bf16[256,32,384]{2,1,0:T(8,128)(2,1)} %hold.2), calls=%async_computation | async-start | bytes 12582912 | tf_op jit(solution)/shard_map/all_to_all | solution.py:628
  93.0 35.6 %collective-permute-start.2 = (bf16[2,64,16,384]{3,2,1,0:T(8,128)(2,1)S(1)}, bf16[2,64,16,384]{3,2,1,0:T(8,128)(2,1)S(1)}, u32[]{:S(2)}, u32[]{:S(2)}) collective-permute-start(bf16[2,64,16,384]{3,2,1,0:T(8,128)(2,1)S(1)} %copy-done.3), channel_id=1, source_target_pairs={{0,16},{8,24},{16,0},{24,8},{1,17},{9,25},{17,1},{25,9},{2,18},{10... | collective-permute-start | bytes 4718600 | tf_op jit(solution)/shard_map/ppermute | solution.py:620
  94.5 41.8 %collective-permute-start.1 = (bf16[2,64,16,384]{3,2,1,0:T(8,128)(2,1)S(1)}, bf16[2,64,16,384]{3,2,1,0:T(8,128)(2,1)}, u32[]{:S(2)}, u32[]{:S(2)}) collective-permute-start(bf16[2,64,16,384]{3,2,1,0:T(8,128)(2,1)S(1)} %copy-done.3), channel_id=1, source_target_pairs={{0,8},{8,0},{16,24},{24,16},{1,9},{9,1},{17,25},{25,17},{2,10},{10... | collective-permute-start | bytes 4718600 | tf_op jit(solution)/shard_map/ppermute | solution.py:620
  128.6 6.3 copy-start.6
  128.6 7.8 collective-permute-start.3
  128.6 6.5 collective-permute-start.6
  134.9 1.3 collective-permute-start.5
  135.0 1.3 copy-start.11
  135.0 1.3 collective-permute-start.7
  136.2 0.7 copy-start.12
  136.3 0.6 copy-start.13
  323.6 3.8 copy-start.16
  323.6 73.8 %all-to-all-start.1 = ((bf16[256,16,384]{2,1,0:T(8,128)(2,1)}), bf16[256,16,384]{2,1,0:T(8,128)(2,1)S(1)}, u32[]{:S(2)}, u32[]{:S(2)}) async-start(bf16[256,16,384]{2,1,0:T(8,128)(2,1)} %bitcast.61), calls=%async_computation.1 | async-start | bytes 6291456 | tf_op jit(solution)/shard_map/all_to_all | solution.py:628
  397.5 1.7 copy-start.4
  399.1 75.5 %all-to-all-start.3 = ((bf16[256,16,384]{2,1,0:T(8,128)(2,1)}), bf16[256,16,384]{2,1,0:T(8,128)(2,1)}, u32[]{:S(2)}, u32[]{:S(2)}) async-start(bf16[256,16,384]{2,1,0:T(8,128)(2,1)} %get-tuple-element.31), calls=%async_computation.3 | async-start | bytes 6291456 | tf_op jit(solution)/shard_map/all_to_all | solution.py:628
  471.7 2.4 copy-start.5
  474.5 6.0 collective-permute-start.8
  474.6 83.6 %all-to-all-start.4 = ((bf16[256,16,384]{2,1,0:T(8,128)(2,1)}), bf16[256,16,384]{2,1,0:T(8,128)(2,1)}, u32[]{:S(2)}, u32[]{:S(2)}) async-start(bf16[256,16,384]{2,1,0:T(8,128)(2,1)} %get-tuple-element.32), calls=%async_computation.4 | async-start | bytes 6291456 | tf_op jit(solution)/shard_map/all_to_all | solution.py:628
  482.2 15.5 %collective-permute-start.9 = (bf16[1,1,2,2,2,24,1536]{6,5,4,3,2,1,0:T(8,128)(2,1)S(1)}, bf16[1,1,2,2,2,24,1536]{6,5,4,3,2,1,0:T(8,128)(2,1)S(1)}, u32[]{:S(2)}, u32[]{:S(2)}) collective-permute-start(bf16[1,1,2,2,2,24,1536]{6,5,4,3,2,1,0:T(8,128)(2,1)S(1)} %constant_dynamic-slice_fusion.6), channel_id=1, source_target_pairs={{0,16},{8,24},{16,0},{24,8},{1,17},{9,25},{17,1},{25,9},{2,18},{10... | collective-permute-start | bytes 1769480 | tf_op jit(solution)/shard_map/ppermute | solution.py:620
  497.9 16.1 %collective-permute-start.10 = (bf16[1,1,2,2,1,24,1536]{6,5,4,3,2,1,0:T(8,128)(2,1)S(1)}, bf16[1,1,2,2,1,24,1536]{6,5,4,3,2,1,0:T(8,128)(2,1)S(1)}, u32[]{:S(2)}, u32[]{:S(2)}) collective-permute-start(bf16[1,1,2,2,1,24,1536]{6,5,4,3,2,1,0:T(8,128)(2,1)S(1)} %constant_dynamic-slice_fusion.5), channel_id=1, source_target_pairs={{0,1},{1,0},{2,3},{3,2},{4,5},{5,4},{6,7},{7,6},{8,9},{9,8},{10,11... | collective-permute-start | bytes 884744 | tf_op jit(solution)/shard_map/ppermute | solution.py:620
  514.1 22.3 %collective-permute-start.11 = (bf16[1,1,2,1,1,24,1536]{6,5,4,3,2,1,0:T(8,128)(2,1)S(1)}, bf16[1,1,2,1,1,24,1536]{6,5,4,3,2,1,0:T(8,128)(2,1)S(1)}, u32[]{:S(2)}, u32[]{:S(2)}) collective-permute-start(bf16[1,1,2,1,1,24,1536]{6,5,4,3,2,1,0:T(8,128)(2,1)S(1)} %constant_dynamic-slice_fusion.4), channel_id=1, source_target_pairs={{0,2},{1,3},{2,0},{3,1},{4,6},{5,7},{6,4},{7,5},{8,10},{9,11},{10,... | collective-permute-start | bytes 442376 | tf_op jit(solution)/shard_map/ppermute | solution.py:620
  536.4 21.1 %collective-permute-start.12 = (bf16[1,1,1,1,1,24,1536]{6,5,4,3,2,1,0:T(8,128)(2,1)S(1)}, bf16[1,1,1,1,1,24,1536]{6,5,4,3,2,1,0:T(8,128)(2,1)S(1)}, u32[]{:S(2)}, u32[]{:S(2)}) collective-permute-start(bf16[1,1,1,1,1,24,1536]{6,5,4,3,2,1,0:T(8,128)(2,1)S(1)} %constant_dynamic-slice_fusion.3), channel_id=1, source_target_pairs={{0,4},{1,5},{2,6},{3,7},{4,0},{5,1},{6,2},{7,3},{8,12},{9,13},{10,... | collective-permute-start | bytes 221192 | tf_op jit(solution)/shard_map/ppermute | solution.py:620
  584.1 6.6 collective-permute-start.13
  584.1 111.2 %all-to-all-start.6 = ((bf16[256,16,384]{2,1,0:T(8,128)(2,1)}), bf16[256,16,384]{2,1,0:T(8,128)(2,1)}, u32[]{:S(2)}, u32[]{:S(2)}) async-start(bf16[256,16,384]{2,1,0:T(8,128)(2,1)} %bitcast.60), calls=%async_computation.6 | async-start | bytes 6291456 | tf_op jit(solution)/shard_map/all_to_all | solution.py:628
  594.3 40.7 %collective-permute-start.14 = (bf16[1,1,18,2,64,384]{5,4,3,2,1,0:T(8,128)(2,1)S(1)}, bf16[1,1,18,2,64,384]{5,4,3,2,1,0:T(8,128)(2,1)S(1)}, u32[]{:S(2)}, u32[]{:S(2)}) collective-permute-start(bf16[1,1,18,2,64,384]{5,4,3,2,1,0:T(8,128)(2,1)S(1)} %constant_dynamic-slice_fusion), channel_id=1, source_target_pairs={{0,16},{8,24},{16,0},{24,8},{1,17},{9,25},{17,1},{25,9},{2,18},{10... | collective-permute-start | bytes 5308424 | tf_op jit(solution)/shard_map/ppermute | solution.py:620
  637.1 42.5 %collective-permute-start.15 = (bf16[16,2,64,384]{3,2,1,0:T(8,128)(2,1)}, bf16[16,2,64,384]{3,2,1,0:T(8,128)(2,1)S(1)}, u32[]{:S(2)}, u32[]{:S(2)}) collective-permute-start(bf16[16,2,64,384]{3,2,1,0:T(8,128)(2,1)} %slice_bitcast_fusion.rest_0_), channel_id=1, source_target_pairs={{0,7},{1,6},{2,5},{3,4},{4,3},{5,2},{6,1},{7,0},{8,15},{9,14},{10,... | collective-permute-start | bytes 4718600 | tf_op jit(solution)/shard_map/ppermute | solution.py:620
  640.4 37.5 %collective-permute-start.16 = (bf16[2,64,384]{2,1,0:T(8,128)(2,1)S(1)}, bf16[2,64,384]{2,1,0:T(8,128)(2,1)S(1)}, u32[]{:S(2)}, u32[]{:S(2)}) collective-permute-start(bf16[2,64,384]{2,1,0:T(8,128)(2,1)S(1)} %fusion.1), channel_id=1, source_target_pairs={{0,4},{1,7},{2,6},{3,5},{8,12},{9,15},{10,14},{11,13},{16,20},{17,... | collective-permute-start | bytes 294920 | tf_op jit(solution)/shard_map/ppermute | solution.py:744
  678.0 1.7 copy-start.7
  679.7 1.1 copy-start.1
  680.8 57.3 %copy-start.8 = (bf16[2,64,384]{2,1,0:T(8,128)(2,1)S(1)}, bf16[2,64,384]{2,1,0:T(8,128)(2,1)}, u32[]{:S(2)}) copy-start(bf16[2,64,384]{2,1,0:T(8,128)(2,1)} %copy-done.7) | copy-start | bytes 294916
  695.4 175.1 %all-to-all-start.5 = ((bf16[256,16,384]{2,1,0:T(8,128)(2,1)}), bf16[256,16,384]{2,1,0:T(8,128)(2,1)S(1)}, u32[]{:S(2)}, u32[]{:S(2)}) async-start(bf16[256,16,384]{2,1,0:T(8,128)(2,1)} %hold.3), calls=%async_computation.5 | async-start | bytes 6291456 | tf_op jit(solution)/shard_map/all_to_all | solution.py:628
  737.4 78.4 %copy-start.14 = (f32[16,384]{1,0:T(8,128)S(1)}, f32[16,384]{1,0:T(8,128)}, u32[]{:S(2)}) copy-start(f32[16,384]{1,0:T(8,128)} %get-tuple-element.38) | copy-start | bytes 73732
  737.4 97.5 %all-gather.3.cloned.1.call-start = ((), (), s32[]{:S(2)}) async-start(), calls=%async_computation.7 | async-start | bytes 2433024 | tf_op jit(solution)/shard_map/all_gather | solution.py:734
  740.9 40.2 %collective-permute-start.21 = (bf16[17,2,64,384]{3,2,1,0:T(8,128)(2,1)}, bf16[17,2,64,384]{3,2,1,0:T(8,128)(2,1)}, u32[]{:S(2)}, u32[]{:S(2)}) collective-permute-start(bf16[17,2,64,384]{3,2,1,0:T(8,128)(2,1)} %pad_maximum_fusion.1.rest_4_), channel_id=1, source_target_pairs={{0,16},{8,24},{16,0},{24,8},{1,17},{9,25},{17,1},{25,9},{2,18},{10... | collective-permute-start | bytes 5013512 | tf_op jit(solution)/shard_map/ppermute | solution.py:620
  742.4 73.3 %collective-permute-start.18 = (bf16[16,2,64,384]{3,2,1,0:T(8,128)(2,1)}, bf16[16,2,64,384]{3,2,1,0:T(8,128)(2,1)}, u32[]{:S(2)}, u32[]{:S(2)}) collective-permute-start(bf16[16,2,64,384]{3,2,1,0:T(8,128)(2,1)} %slice_bitcast_fusion.rest_0_), channel_id=1, source_target_pairs={{0,16},{8,24},{16,0},{24,8},{1,17},{9,25},{17,1},{25,9},{2,18},{10... | collective-permute-start | bytes 4718600 | tf_op jit(solution)/shard_map/ppermute | solution.py:620
  743.0 109.1 %collective-permute-start.20 = (bf16[17,2,64,384]{3,2,1,0:T(8,128)(2,1)}, bf16[17,2,64,384]{3,2,1,0:T(8,128)(2,1)}, u32[]{:S(2)}, u32[]{:S(2)}) collective-permute-start(bf16[17,2,64,384]{3,2,1,0:T(8,128)(2,1)} %pad_maximum_fusion.1.rest_4_), channel_id=1, source_target_pairs={{0,8},{8,0},{16,24},{24,16},{1,9},{9,1},{17,25},{25,17},{2,10},{10... | collective-permute-start | bytes 5013512 | tf_op jit(solution)/shard_map/ppermute | solution.py:620
  781.2 70.9 %collective-permute-start.22 = (bf16[17,2,64,384]{3,2,1,0:T(8,128)(2,1)}, bf16[17,2,64,384]{3,2,1,0:T(8,128)(2,1)}, u32[]{:S(2)}, u32[]{:S(2)}) collective-permute-start(bf16[17,2,64,384]{3,2,1,0:T(8,128)(2,1)} %collective-permute-done.21.rest_6_), channel_id=1, source_target_pairs={{0,8},{8,0},{16,24},{24,16},{1,9},{9,1},{17,25},{25,17},{2,10},{10... | collective-permute-start | bytes 5013512 | tf_op jit(solution)/shard_map/ppermute | solution.py:620
  781.2 70.9 %collective-permute-start.17 = (bf16[16,2,64,384]{3,2,1,0:T(8,128)(2,1)}, bf16[16,2,64,384]{3,2,1,0:T(8,128)(2,1)}, u32[]{:S(2)}, u32[]{:S(2)}) collective-permute-start(bf16[16,2,64,384]{3,2,1,0:T(8,128)(2,1)} %slice_bitcast_fusion.rest_0_), channel_id=1, source_target_pairs={{0,8},{8,0},{16,24},{24,16},{1,9},{9,1},{17,25},{25,17},{2,10},{10... | collective-permute-start | bytes 4718600 | tf_op jit(solution)/shard_map/ppermute | solution.py:620
  815.8 36.3 %collective-permute-start.19 = (bf16[16,2,64,384]{3,2,1,0:T(8,128)(2,1)}, bf16[16,2,64,384]{3,2,1,0:T(8,128)(2,1)}, u32[]{:S(2)}, u32[]{:S(2)}) collective-permute-start(bf16[16,2,64,384]{3,2,1,0:T(8,128)(2,1)} %collective-permute-done.18.rest_2_), channel_id=1, source_target_pairs={{0,8},{8,0},{16,24},{24,16},{1,9},{9,1},{17,25},{25,17},{2,10},{10... | collective-permute-start | bytes 4718600 | tf_op jit(solution)/shard_map/ppermute | solution.py:620
  815.8 3.0 collective-permute-start.23
  818.8 3.7 collective-permute-start.24
  822.5 3.7 collective-permute-start.25
  826.2 3.6 collective-permute-start.26
  829.8 4.5 collective-permute-start.27
  870.4 1.6 copy-start
Sparse Core Ops, SparseCore 0:
  741.7 92.1 all-gather.2
where the time goes:
time: 898 us; the launch traced here: 891 us
  waiting for transfers between devices  394 us (44%)
  Pallas kernels  248 us (28%)
  starting transfers between devices  117 us (13%)
  blocking collectives  74.7 us (8%)
  local copies, waits for them, and re-layouts  30.6 us (3%)
  between operations  14.6 us (2%)
  other arithmetic  12.3 us (1%)
    ppermute x26, waiting for transfers between devices, swap(): return lax.ppermute(value, axis, [(i, partner(i)) for i in range(size)])  212 us
    pallas_call x2, Pallas kernels, mlp(): pl.pallas_call(functools.partial(mlp_kernel, n, previous is not None), gr...  135 us
    all_to_all x6, waiting for transfers between devices, exchange(): lax.all_to_all(value, 'space', split_axis=0, concat_axis=0, tiled=True)  96 us
    all_to_all x1, blocking collectives, exchange(): lax.all_to_all(value, 'space', split_axis=0, concat_axis=0, tiled=True)  74.7 us
    all_to_all x6, starting transfers between devices, exchange(): lax.all_to_all(value, 'space', split_axis=0, concat_axis=0, tiled=True)  66.3 us
    ppermute x1, waiting for transfers between devices, body(): single = lax.ppermute(single.reshape(2, share, chans), 'space', to_lower)  49.3 us
    ppermute x26, starting transfers between devices, swap(): return lax.ppermute(value, axis, [(i, partner(i)) for i in range(size)])  47.5 us
    pallas_call x2, Pallas kernels, columns(): pl.pallas_call(functools.partial(columns_kernel, count, outs, back), grid...  37.8 us
  transfers between devices with their start and end apart: 35, of which 22 were waited for; matrix products, arithmetic and copies ran while one was open for 3% of the time, Pallas kernels for 22%

commit v1 on v0

--- a/solution.py
+++ b/solution.py
@@ -729,7 +729,7 @@
     gains = gains * factor
 
     returned, terms = columns(
-        flags(copy), (backward_in, out_tabs), kernel, arrived, chunks, spectrum, (part,)
+        flags(copy), (backward_in, out_tabs), kernel, arrived, chunks, spectrum, (part, gains)
     )
     grads = lax.all_gather(part, axes, tiled=True)
     received = exchange(join(returned[0]))
@@ -745,10 +745,10 @@
         jnp.where(me == 0, reduced[half], reduced[half - 1]), "space", to_upper
     )
     mine = gather_copies(reduced[:half], copies)
-    received = exchange(hold(join(returned[1]), (mirrored, single)))
+    received = exchange(hold(join(returned[1]), (mirrored, single, *mine, grad_tokens)))
     theirs = gather_copies(jnp.concatenate([mirrored, single[None]], axis=0), copies)
     grad_filter = filter_gradient(
-        flags(copy), mirror, mine, theirs, height, wide, (grad_tokens,)
+        flags(copy), mirror, mine, theirs, height, wide, ()
     )
     grad_tokens = leave(
         [received], tokens, upstream, gain_a, table_out, grad_tokens, 1, 2, (grad_filter,)

time: 898 us -> 946 us (1.053)
  waiting for transfers between devices: 394 us -> 472 us
  starting transfers between devices: 117 us -> 87.8 us
    all_to_all x6, waiting for transfers between devices: 96 us -> 169 us  [exchange(): lax.all_to_all(value, 'space', split_axis=0, concat_axis=0, tiled=True)]
    all_gather x1, waiting for transfers between devices: 0.01 us -> 53.3 us  [body(): grads = lax.all_gather(part, axes, tiled=True)]
    ppermute x1, waiting for transfers between devices: 36 us -> 0.01 us  [body(): lax.ppermute(jnp.where(me == 0, reduced[half], reduced[half - 1]), 'space...]
    ppermute x26, starting transfers between devices: 47.5 us -> 31.9 us  [swap(): return lax.ppermute(value, axis, [(i, partner(i)) for i in range(size)])]
    all_to_all x6, starting transfers between devices: 66.3 us -> 51.8 us  [exchange(): lax.all_to_all(value, 'space', split_axis=0, concat_axis=0, tiled=True)]
    ppermute x26, waiting for transfers between devices: 212 us -> 200 us  [swap(): return lax.ppermute(value, axis, [(i, partner(i)) for i in range(size)])]
  transfers between devices with their start and end apart: 35 -> 35, of which waited for: 22 -> 20; matrix products, arithmetic and copies ran while one was open for 3% -> 3% of each run, Pallas kernels for 22% -> 14%
where the time goes in v1:
time: 946 us; the launch traced here: 939 us
  waiting for transfers between devices  472 us (50%)
  Pallas kernels  248 us (26%)
  starting transfers between devices  87.8 us (9%)
  blocking collectives  74.7 us (8%)
  local copies, waits for them, and re-layouts  28.6 us (3%)
  between operations  14.7 us (2%)
  other arithmetic  13.5 us (1%)
    ppermute x26, waiting for transfers between devices, swap(): return lax.ppermute(value, axis, [(i, partner(i)) for i in range(size)])  200 us
    all_to_all x6, waiting for transfers between devices, exchange(): lax.all_to_all(value, 'space', split_axis=0, concat_axis=0, tiled=True)  169 us
    pallas_call x2, Pallas kernels, mlp(): pl.pallas_call(functools.partial(mlp_kernel, n, previous is not None), gr...  135 us
    all_to_all x1, blocking collectives, exchange(): lax.all_to_all(value, 'space', split_axis=0, concat_axis=0, tiled=True)  74.7 us
    all_gather x1, waiting for transfers between devices, body(): grads = lax.all_gather(part, axes, tiled=True)  53.3 us
    all_to_all x6, starting transfers between devices, exchange(): lax.all_to_all(value, 'space', split_axis=0, concat_axis=0, tiled=True)  51.8 us
    ppermute x1, waiting for transfers between devices, body(): single = lax.ppermute(single.reshape(2, share, chans), 'space', to_lower)  49.3 us
    pallas_call x2, Pallas kernels, columns(): pl.pallas_call(functools.partial(columns_kernel, count, outs, back), grid...  37.8 us
  transfers between devices with their start and end apart: 35, of which 20 were waited for; matrix products, arithmetic and copies ran while one was open for 3% of the time, Pallas kernels for 14%

profile of v1, /device:TPU:0, one launch (start us, length us, event | category | flops | bytes accessed | tf_op | source)
XLA Modules:
  0.0 938.9 jit_solution(5458202917134352940)
XLA Ops:
  7.2 1.6 constant_dynamic-slice_fusion.9
  8.8 6.1 collective-permute-start
  14.8 1.3 constant_dynamic-slice_fusion.8
  16.1 1.3 collective-permute-start.4
  18.0 19.0 %enter_rows.1.refs_0_ = bf16[256,32,384]{2,1,0:T(8,128)(2,1)} custom-call(bf16[32,256,384]{2,1,0:T(8,128)(2,1)} %bitcast.40, f32[1,384]{1,0:T(1,128)} %reshape.65.gain, bf16[256,256]{1,0:T(8,128)(2,1)} %constant.87.clone.table.table_in), custom_call_target="tpu_custom_call" | custom-call | flops 1610612736 | bytes 12582912 | tf_op jit(solution)/shard_map/enter_rows/pallas_call | solution.py:208
  37.0 49.3 %collective-permute-done.4.rest_4_.refs_2_ = bf16[2,64,384]{2,1,0:T(8,128)(2,1)S(1)} collective-permute-done((bf16[2,64,384]{2,1,0:T(8,128)(2,1)S(1)}, bf16[2,64,384]{2,1,0:T(8,128)(2,1)S(1)}, u32[]{:S(2)}, u32[]{:S(2)}) %collective-permute-start.4) | collective-permute-done | bytes 98336 | tf_op jit(solution)/shard_map/ppermute | solution.py:677
  87.0 1.1 copy-done.3
  88.1 5.0 all-to-all-start
  93.1 1.6 collective-permute-start.2
  94.7 34.0 %collective-permute-done.2.rest_2_ = bf16[2,64,16,384]{3,2,1,0:T(8,128)(2,1)S(1)} collective-permute-done((bf16[2,64,16,384]{3,2,1,0:T(8,128)(2,1)S(1)}, bf16[2,64,16,384]{3,2,1,0:T(8,128)(2,1)S(1)}, u32[]{:S(2)}, u32[]{:S(2)}) %collective-permute-start.2) | collective-permute-done | bytes 1572896 | tf_op jit(solution)/shard_map/ppermute | solution.py:620
  128.7 1.6 collective-permute-start.6
  130.2 2.4 copy.27
  132.6 2.4 copy.28
  137.1 15.4 %filter_part.1.kernel = bf16[18,2,256,384]{3,2,1,0:T(8,128)(2,1)} custom-call(s32[3]{0:T(128)} %pad_add_fusion.flags, bf16[256,256]{1,0:T(8,128)(2,1)} %constant.92.clone.mirror, bf16[2,256,32,384]{3,2,1,0:T(8,128)(2,1)} %own.1, bf16[2,64,16,384]{3,2,1,0:T(8,128)(2,1)} %copy-done.3, bf16[2,64,16,384]{3,2,1,0:T(8,128)(2,1)} %collective-permute-done.1.rest_1_, ...), custom_call_target="tpu_custom_call" | custom-call | flops 1610612736 | bytes 25165824 | tf_op jit(solution)/shard_map/filter_part/pallas_call | solution.py:521
  152.5 78.4 %all-to-all-done = bf16[256,32,384]{2,1,0:T(8,128)(2,1)} async-done(((bf16[256,32,384]{2,1,0:T(8,128)(2,1)}), bf16[256,32,384]{2,1,0:T(8,128)(2,1)}, u32[]{:S(2)}, u32[]{:S(2)}) %all-to-all-start) | async-done | bytes 6291488 | tf_op jit(solution)/shard_map/all_to_all | solution.py:628
  230.9 18.1 %filter_columns.2 = (bf16[8,2,16,16,384]{4,3,2,1,0:T(8,128)(2,1)}, bf16[8,2,16,16,384]{4,3,2,1,0:T(8,128)(2,1)}, bf16[18,2,256,384]{3,2,1,0:T(8,128)(2,1)}) custom-call(s32[3]{0:T(128)} %pad_add_fusion.flags, bf16[3,512,512]{2,1,0:T(8,128)(2,1)} %constant.89.clone.table_f, bf16[3,512,512]{2,1,0:T(8,128)(2,1)} %constant.91.clone.table_b, ...), custom_call_target="tpu_custom_call" | custom-call | flops 7247757312 | bytes 35389440 | tf_op jit(solution)/shard_map/filter_columns/pallas_call | solution.py:444
  249.0 74.7 %all_to_all.35.rest_0_ = bf16[256,16,384]{2,1,0:T(8,128)(2,1)} all-to-all(bf16[256,16,384]{2,1,0:T(8,128)(2,1)} %bitcast.62), channel_id=1, replica_groups=mesh['copy'=4,'space'=8] {'space'}, dimensions={0} | all-to-all | bytes 6291456 | tf_op jit(solution)/shard_map/all_to_all | solution.py:628
  323.7 3.8 all-to-all-start.1
  328.1 66.5 %mlp_rows.2 = (bf16[32,256,384]{2,1,0:T(8,128)(2,1)}, bf16[256,16,384]{2,1,0:T(8,128)(2,1)}, f32[384,1536]{1,0:T(8,128)}, f32[384,1536]{1,0:T(8,128)}, f32[16,384]{1,0:T(8,128)}) custom-call(bf16[32,256,384]{2,1,0:T(8,128)(2,1)} %bitcast.41, bf16[32,256,384]{2,1,0:T(8,128)(2,1)} %bitcast.46, f32[1,384]{1,0:T(1,128)} %reshape.63.gain, ...), custom_call_target="tpu_custom_call" | custom-call | flops 30601641984 | bytes 15728640 | tf_op jit(solution)/shard_map/mlp_rows/pallas_call | solution.py:313
  394.6 2.9 all-to-all-done.1.rest_0_
  397.5 1.7 copy-done.5
  399.2 68.2 %mlp_rows.3 = (bf16[32,256,384]{2,1,0:T(8,128)(2,1)}, bf16[256,16,384]{2,1,0:T(8,128)(2,1)}, f32[384,1536]{1,0:T(8,128)}, f32[384,1536]{1,0:T(8,128)}, f32[16,384]{1,0:T(8,128)}) custom-call(bf16[32,256,384]{2,1,0:T(8,128)(2,1)} %bitcast.42, bf16[32,256,384]{2,1,0:T(8,128)(2,1)} %bitcast.47, ...), custom_call_target="tpu_custom_call", output_to_operand_aliasing={{0}: (10, {})} | custom-call | flops 30601641984 | bytes 15728640 | tf_op jit(solution)/shard_map/mlp_rows/pallas_call | solution.py:313
  467.4 4.5 all-to-all-start.4
  471.9 1.9 convert.10
  474.8 67.3 %all-to-all-done.4 = bf16[256,16,384]{2,1,0:T(8,128)(2,1)} async-done(((bf16[256,16,384]{2,1,0:T(8,128)(2,1)}), bf16[256,16,384]{2,1,0:T(8,128)(2,1)}, u32[]{:S(2)}, u32[]{:S(2)}) %all-to-all-start.4) | async-done | bytes 3145760 | tf_op jit(solution)/shard_map/all_to_all | solution.py:628
  542.1 4.4 all-to-all-start.3
  546.6 1.6 add_convert_fusion.1
  548.2 1.5 collective-permute-start.9
  549.8 0.7 slice_reduce_fusion.1
  550.6 11.9 %collective-permute-done.9 = bf16[1,1,2,2,2,24,1536]{6,5,4,3,2,1,0:T(8,128)(2,1)S(1)} collective-permute-done((bf16[1,1,2,2,2,24,1536]{6,5,4,3,2,1,0:T(8,128)(2,1)S(1)}, bf16[1,1,2,2,2,24,1536]{6,5,4,3,2,1,0:T(8,128)(2,1)S(1)}, u32[]{:S(2)}, u32[]{:S(2)}) %collective-permute-start.9) | collective-permute-done | bytes 589856 | tf_op jit(solution)/shard_map/ppermute | solution.py:620
  562.6 1.8 collective-permute-start.10
  564.5 1.1 collective-permute-done.13
  565.7 1.5 collective-permute-start.14
  567.2 11.9 %collective-permute-done.10 = bf16[1,1,2,2,1,24,1536]{6,5,4,3,2,1,0:T(8,128)(2,1)S(1)} collective-permute-done((bf16[1,1,2,2,1,24,1536]{6,5,4,3,2,1,0:T(8,128)(2,1)S(1)}, bf16[1,1,2,2,1,24,1536]{6,5,4,3,2,1,0:T(8,128)(2,1)S(1)}, u32[]{:S(2)}, u32[]{:S(2)}) %collective-permute-start.10) | collective-permute-done | bytes 294944 | tf_op jit(solution)/shard_map/ppermute | solution.py:620
  579.6 2.6 collective-permute-start.15
  582.1 1.6 collective-permute-done.15
  583.8 2.0 collective-permute-start.16
  585.7 14.9 %collective-permute-done.16 = f32[2,384]{1,0:T(2,128)S(1)} collective-permute-done((f32[2,384]{1,0:T(2,128)S(1)}, f32[2,384]{1,0:T(2,128)S(1)}, u32[]{:S(2)}, u32[]{:S(2)}) %collective-permute-start.16) | collective-permute-done | bytes 3104 | tf_op jit(solution)/shard_map/ppermute | solution.py:620
  600.7 5.0 collective-permute-start.17
  605.9 13.3 %collective-permute-done.17 = f32[2,384]{1,0:T(2,128)S(1)} collective-permute-done((f32[2,384]{1,0:T(2,128)S(1)}, f32[2,384]{1,0:T(2,128)S(1)}, u32[]{:S(2)}, u32[]{:S(2)}) %collective-permute-start.17) | collective-permute-done | bytes 3104 | tf_op jit(solution)/shard_map/ppermute | solution.py:620
  620.6 19.7 %filter_columns.3 = (bf16[8,2,16,16,384]{4,3,2,1,0:T(8,128)(2,1)}, bf16[8,2,16,16,384]{4,3,2,1,0:T(8,128)(2,1)}, bf16[18,2,256,384]{3,2,1,0:T(8,128)(2,1)}) custom-call(s32[3]{0:T(128)} %pad_add_fusion.flags, bf16[3,512,512]{2,1,0:T(8,128)(2,1)} %constant.90.clone.table_f, bf16[3,512,512]{2,1,0:T(8,128)(2,1)} %constant.91.clone.table_b, ...), custom_call_target="tpu_custom_call" | custom-call | flops 7247757312 | bytes 35389440 | tf_op jit(solution)/shard_map/filter_columns/pallas_call | solution.py:444
  640.2 4.1 constant_dynamic-slice_fusion.2
  644.3 2.2 copy.39
  646.5 4.5 all-to-all-start.5
  651.0 2.1 collective-permute-done.18
  653.1 3.3 fusion
  656.7 1.5 collective-permute-start.19
  658.2 39.2 %collective-permute-done.19 = bf16[1,1,18,2,64,384]{5,4,3,2,1,0:T(8,128)(2,1)S(1)} collective-permute-done((bf16[1,1,18,2,64,384]{5,4,3,2,1,0:T(8,128)(2,1)S(1)}, bf16[1,1,18,2,64,384]{5,4,3,2,1,0:T(8,128)(2,1)S(1)}, u32[]{:S(2)}, u32[]{:S(2)}) %collective-permute-start.19) | collective-permute-done | bytes 1769504 | tf_op jit(solution)/shard_map/ppermute | solution.py:620
  698.3 1.5 collective-permute-start.23
  699.8 2.6 collective-permute-start.20
  702.5 31.6 %collective-permute-done.23.refs_5_.rest_2_ = bf16[16,2,64,384]{3,2,1,0:T(8,128)(2,1)S(1)} collective-permute-done((bf16[16,2,64,384]{3,2,1,0:T(8,128)(2,1)S(1)}, bf16[16,2,64,384]{3,2,1,0:T(8,128)(2,1)S(1)}, u32[]{:S(2)}, u32[]{:S(2)}) %collective-permute-start.23) | collective-permute-done | bytes 1572896 | tf_op jit(solution)/shard_map/ppermute | solution.py:620
  734.1 2.7 collective-permute-start.21
  736.8 19.9 %all-to-all-done.5.rest_0_ = bf16[256,16,384]{2,1,0:T(8,128)(2,1)} async-done(((bf16[256,16,384]{2,1,0:T(8,128)(2,1)}), bf16[256,16,384]{2,1,0:T(8,128)(2,1)}, u32[]{:S(2)}, u32[]{:S(2)}) %all-to-all-start.5) | async-done | bytes 3145760 | tf_op jit(solution)/shard_map/all_to_all | solution.py:628
  756.8 11.4 %leave_rows.2.refs_7_.rest_1_ = bf16[32,256,384]{2,1,0:T(8,128)(2,1)} custom-call(bf16[32,256,384]{2,1,0:T(8,128)(2,1)} %bitcast.43, bf16[32,256,384]{2,1,0:T(8,128)(2,1)} %bitcast.48, f32[1,384]{1,0:T(1,128)} %reshape.65.gain, bf16[256,256]{1,0:T(8,128)(2,1)} %constant.88.clone.table_out, bf16[256,16,384]{2,1,0:T(8,128)(2,1)} %all-to-all-done.5.rest_0_), custom_call_target="tpu_custom_call" | custom-call | flops 805306368 | bytes 12582912 | tf_op jit(solution)/shard_map/leave_rows/pallas_call | solution.py:369
  768.8 29.7 %all-to-all-start.6 = ((bf16[256,16,384]{2,1,0:T(8,128)(2,1)}), bf16[256,16,384]{2,1,0:T(8,128)(2,1)S(1)}, u32[]{:S(2)}, u32[]{:S(2)}) async-start(bf16[256,16,384]{2,1,0:T(8,128)(2,1)} %hold.3), calls=%async_computation.6 | async-start | bytes 6291456 | tf_op jit(solution)/shard_map/all_to_all | solution.py:628
  799.3 2.8 pad_maximum_fusion.1.rest_4_
  802.1 1.5 collective-permute-start.26
  803.5 37.6 %collective-permute-done.26.rest_6_ = bf16[17,2,64,384]{3,2,1,0:T(8,128)(2,1)} collective-permute-done((bf16[17,2,64,384]{3,2,1,0:T(8,128)(2,1)}, bf16[17,2,64,384]{3,2,1,0:T(8,128)(2,1)}, u32[]{:S(2)}, u32[]{:S(2)}) %collective-permute-start.26) | collective-permute-done | bytes 1671200 | tf_op jit(solution)/shard_map/ppermute | solution.py:620
  841.7 53.3 %all-gather.3.cloned.1.call-done = bf16[1,1,1,1,1,768,1536]{6,5,4,3,2,1,0:T(8,128)(2,1)} async-done(((bf16[1,1,1,1,1,24,1536]{6,5,4,3,2,1,0:T(8,128)(2,1)}), bf16[1,1,1,1,1,768,1536]{6,5,4,3,2,1,0:T(8,128)(2,1)}) %all-gather.3.cloned.1.call-update) | async-done | bytes 2359312 | tf_op jit(solution)/shard_map/all_gather | solution.py:734
  895.0 3.2 slice_bitcast_fusion.1
  898.2 2.4 copy.32
  900.5 18.3 %filter_gradient.1.rest_2_ = f32[2,256,32,384]{3,2,1,0:T(8,128)} custom-call(s32[3]{0:T(128)} %pad_add_fusion.flags, bf16[256,256]{1,0:T(8,128)(2,1)} %constant.92.clone.mirror, bf16[16,2,64,384]{3,2,1,0:T(8,128)(2,1)} %copy-done, bf16[16,2,64,384]{3,2,1,0:T(8,128)(2,1)} %collective-permute-done.22.refs_4_.rest_1_, bf16[16,2,64,384]{3,2,1,0:T(8,128)(2,1)} %copy-done.2, ...), custom_call_target="tpu_custom_call" | custom-call | flops 1610612736 | bytes 37748736 | tf_op jit(solution)/shard_map/filter_gradient/pallas_call | solution.py:597
  918.9 1.6 copy-done.1
  920.5 11.4 %leave_rows.3 = bf16[32,256,384]{2,1,0:T(8,128)(2,1)} custom-call(bf16[32,256,384]{2,1,0:T(8,128)(2,1)} %bitcast.44, bf16[32,256,384]{2,1,0:T(8,128)(2,1)} %bitcast.49, f32[1,384]{1,0:T(1,128)} %reshape.65.gain, bf16[256,256]{1,0:T(8,128)(2,1)} %constant.88.clone.table_out, bf16[256,16,384]{2,1,0:T(8,128)(2,1)} %copy-done.1, ...), custom_call_target="tpu_custom_call", output_to_operand_aliasing={{}: (5, {})} | custom-call | flops 805306368 | bytes 12582912 | tf_op jit(solution)/shard_map/leave_rows/pallas_call | solution.py:369
  (97 shorter events, 10.2 us)
Async XLA Ops:
  7.2 10.3 %copy-start.16 = (f32[384]{0:T(512)S(1)}, f32[384]{0:T(512)}, u32[]{:S(2)}) copy-start(f32[384]{0:T(512)} %param.18) | copy-start | bytes 4612
  8.8 77.5 %collective-permute-start = (bf16[2,64,16,384]{3,2,1,0:T(8,128)(2,1)S(1)}, bf16[2,64,16,384]{3,2,1,0:T(8,128)(2,1)S(1)}, u32[]{:S(2)}, u32[]{:S(2)}) collective-permute-start(bf16[2,64,16,384]{3,2,1,0:T(8,128)(2,1)S(1)} %constant_dynamic-slice_fusion.9), channel_id=1, source_target_pairs={{0,7},{1,6},{2,5},{3,4},{4,3},{5,2},{6,1},{7,0},{8,15},{9,14},{10,... | collective-permute-start | bytes 4718600 | tf_op jit(solution)/shard_map/ppermute | solution.py:620
  16.1 70.2 %collective-permute-start.4 = (bf16[2,64,384]{2,1,0:T(8,128)(2,1)S(1)}, bf16[2,64,384]{2,1,0:T(8,128)(2,1)S(1)}, u32[]{:S(2)}, u32[]{:S(2)}) collective-permute-start(bf16[2,64,384]{2,1,0:T(8,128)(2,1)S(1)} %bitcast.65), channel_id=1, source_target_pairs={{4,0},{5,3},{6,2},{7,1},{12,8},{13,11},{14,10},{15,9},{20,16},{21,... | collective-permute-start | bytes 294920 | tf_op jit(solution)/shard_map/ppermute | solution.py:677
  86.3 0.6 copy-start.10
  87.0 1.1 copy-start.3
  88.1 5.0 copy-start.4
  88.1 40.6 %copy-start.11 = (bf16[2,64,384]{2,1,0:T(8,128)(2,1)S(1)}, bf16[2,64,384]{2,1,0:T(8,128)(2,1)}, u32[]{:S(2)}) copy-start(bf16[2,64,384]{2,1,0:T(8,128)(2,1)} %copy-done.10) | copy-start | bytes 294916
  88.1 142.8 %all-to-all-start = ((bf16[256,32,384]{2,1,0:T(8,128)(2,1)}), bf16[256,32,384]{2,1,0:T(8,128)(2,1)}, u32[]{:S(2)}, u32[]{:S(2)}) async-start(bf16[256,32,384]{2,1,0:T(8,128)(2,1)} %hold.2), calls=%async_computation | async-start | bytes 12582912 | tf_op jit(solution)/shard_map/all_to_all | solution.py:628
  93.1 35.6 %collective-permute-start.2 = (bf16[2,64,16,384]{3,2,1,0:T(8,128)(2,1)S(1)}, bf16[2,64,16,384]{3,2,1,0:T(8,128)(2,1)S(1)}, u32[]{:S(2)}, u32[]{:S(2)}) collective-permute-start(bf16[2,64,16,384]{3,2,1,0:T(8,128)(2,1)S(1)} %copy-done.4), channel_id=1, source_target_pairs={{0,16},{8,24},{16,0},{24,8},{1,17},{9,25},{17,1},{25,9},{2,18},{10... | collective-permute-start | bytes 4718600 | tf_op jit(solution)/shard_map/ppermute | solution.py:620
  94.6 41.8 %collective-permute-start.1 = (bf16[2,64,16,384]{3,2,1,0:T(8,128)(2,1)S(1)}, bf16[2,64,16,384]{3,2,1,0:T(8,128)(2,1)}, u32[]{:S(2)}, u32[]{:S(2)}) collective-permute-start(bf16[2,64,16,384]{3,2,1,0:T(8,128)(2,1)S(1)} %copy-done.4), channel_id=1, source_target_pairs={{0,8},{8,0},{16,24},{24,16},{1,9},{9,1},{17,25},{25,17},{2,10},{10... | collective-permute-start | bytes 4718600 | tf_op jit(solution)/shard_map/ppermute | solution.py:620
  128.7 6.3 copy-start.7
  128.7 7.8 collective-permute-start.3
  128.7 6.5 collective-permute-start.6
  135.0 1.3 collective-permute-start.5
  135.1 1.3 copy-start.12
  135.1 1.3 collective-permute-start.7
  136.3 0.6 copy-start.13
  136.4 0.6 copy-start.14
  323.7 3.8 copy-start.17
  323.7 73.8 %all-to-all-start.1 = ((bf16[256,16,384]{2,1,0:T(8,128)(2,1)}), bf16[256,16,384]{2,1,0:T(8,128)(2,1)S(1)}, u32[]{:S(2)}, u32[]{:S(2)}) async-start(bf16[256,16,384]{2,1,0:T(8,128)(2,1)} %bitcast.61), calls=%async_computation.1 | async-start | bytes 6291456 | tf_op jit(solution)/shard_map/all_to_all | solution.py:628
  397.5 1.7 copy-start.5
  467.4 74.6 %all-to-all-start.4 = ((bf16[256,16,384]{2,1,0:T(8,128)(2,1)}), bf16[256,16,384]{2,1,0:T(8,128)(2,1)}, u32[]{:S(2)}, u32[]{:S(2)}) async-start(bf16[256,16,384]{2,1,0:T(8,128)(2,1)} %get-tuple-element.32), calls=%async_computation.4 | async-start | bytes 6291456 | tf_op jit(solution)/shard_map/all_to_all | solution.py:628
  471.9 2.4 copy-start.6
  474.7 71.8 %collective-permute-start.8 = (bf16[2,1,2,2,2,24,1536]{6,5,4,3,2,1,0:T(8,128)(2,1)S(1)}, bf16[2,1,2,2,2,24,1536]{6,5,4,3,2,1,0:T(8,128)(2,1)}, u32[]{:S(2)}, u32[]{:S(2)}) collective-permute-start(bf16[2,1,2,2,2,24,1536]{6,5,4,3,2,1,0:T(8,128)(2,1)S(1)} %constant_dynamic-slice_fusion.7), channel_id=1, source_target_pairs={{0,8},{8,0},{16,24},{24,16},{1,9},{9,1},{17,25},{25,17},{2,10},{10... | collective-permute-start | bytes 3538952 | tf_op jit(solution)/shard_map/ppermute | solution.py:620
  542.1 78.5 %all-to-all-start.3 = ((bf16[256,16,384]{2,1,0:T(8,128)(2,1)}), bf16[256,16,384]{2,1,0:T(8,128)(2,1)}, u32[]{:S(2)}, u32[]{:S(2)}) async-start(bf16[256,16,384]{2,1,0:T(8,128)(2,1)} %get-tuple-element.31), calls=%async_computation.3 | async-start | bytes 6291456 | tf_op jit(solution)/shard_map/all_to_all | solution.py:628
  548.2 14.2 %collective-permute-start.9 = (bf16[1,1,2,2,2,24,1536]{6,5,4,3,2,1,0:T(8,128)(2,1)S(1)}, bf16[1,1,2,2,2,24,1536]{6,5,4,3,2,1,0:T(8,128)(2,1)S(1)}, u32[]{:S(2)}, u32[]{:S(2)}) collective-permute-start(bf16[1,1,2,2,2,24,1536]{6,5,4,3,2,1,0:T(8,128)(2,1)S(1)} %constant_dynamic-slice_fusion.6), channel_id=1, source_target_pairs={{0,16},{8,24},{16,0},{24,8},{1,17},{9,25},{17,1},{25,9},{2,18},{10... | collective-permute-start | bytes 1769480 | tf_op jit(solution)/shard_map/ppermute | solution.py:620
  562.6 16.5 %collective-permute-start.10 = (bf16[1,1,2,2,1,24,1536]{6,5,4,3,2,1,0:T(8,128)(2,1)S(1)}, bf16[1,1,2,2,1,24,1536]{6,5,4,3,2,1,0:T(8,128)(2,1)S(1)}, u32[]{:S(2)}, u32[]{:S(2)}) collective-permute-start(bf16[1,1,2,2,1,24,1536]{6,5,4,3,2,1,0:T(8,128)(2,1)S(1)} %constant_dynamic-slice_fusion.5), channel_id=1, source_target_pairs={{0,1},{1,0},{2,3},{3,2},{4,5},{5,4},{6,7},{7,6},{8,9},{9,8},{10,11... | collective-permute-start | bytes 884744 | tf_op jit(solution)/shard_map/ppermute | solution.py:620
  564.4 1.2 collective-permute-start.13
  565.7 13.9 %collective-permute-start.14 = (f32[2,384]{1,0:T(2,128)S(1)}, f32[2,384]{1,0:T(2,128)S(1)}, u32[]{:S(2)}, u32[]{:S(2)}) collective-permute-start(f32[2,384]{1,0:T(2,128)S(1)} %fusion.2), channel_id=1, source_target_pairs={{0,16},{8,24},{16,0},{24,8},{1,17},{9,25},{17,1},{25,9},{2,18},{10... | collective-permute-start | bytes 9224 | tf_op jit(solution)/shard_map/ppermute | solution.py:620
  579.3 26.5 %collective-permute-start.11 = (bf16[1,1,2,1,1,24,1536]{6,5,4,3,2,1,0:T(8,128)(2,1)S(1)}, bf16[1,1,2,1,1,24,1536]{6,5,4,3,2,1,0:T(8,128)(2,1)S(1)}, u32[]{:S(2)}, u32[]{:S(2)}) collective-permute-start(bf16[1,1,2,1,1,24,1536]{6,5,4,3,2,1,0:T(8,128)(2,1)S(1)} %constant_dynamic-slice_fusion.4), channel_id=1, source_target_pairs={{0,2},{1,3},{2,0},{3,1},{4,6},{5,7},{6,4},{7,5},{8,10},{9,11},{10,... | collective-permute-start | bytes 442376 | tf_op jit(solution)/shard_map/ppermute | solution.py:620
  579.6 4.2 collective-permute-start.15
  583.8 16.9 %collective-permute-start.16 = (f32[2,384]{1,0:T(2,128)S(1)}, f32[2,384]{1,0:T(2,128)S(1)}, u32[]{:S(2)}, u32[]{:S(2)}) collective-permute-start(f32[2,384]{1,0:T(2,128)S(1)} %add.104), channel_id=1, source_target_pairs={{0,2},{1,3},{2,0},{3,1},{4,6},{5,7},{6,4},{7,5},{8,10},{9,11},{10,... | collective-permute-start | bytes 9224 | tf_op jit(solution)/shard_map/ppermute | solution.py:620
  600.7 18.5 %collective-permute-start.17 = (f32[2,384]{1,0:T(2,128)S(1)}, f32[2,384]{1,0:T(2,128)S(1)}, u32[]{:S(2)}, u32[]{:S(2)}) collective-permute-start(f32[2,384]{1,0:T(2,128)S(1)} %add.105), channel_id=1, source_target_pairs={{0,4},{1,5},{2,6},{3,7},{4,0},{5,1},{6,2},{7,3},{8,12},{9,13},{10,... | collective-permute-start | bytes 9224 | tf_op jit(solution)/shard_map/ppermute | solution.py:620
  605.8 14.1 %collective-permute-start.12 = (bf16[1,1,1,1,1,24,1536]{6,5,4,3,2,1,0:T(8,128)(2,1)S(1)}, bf16[1,1,1,1,1,24,1536]{6,5,4,3,2,1,0:T(8,128)(2,1)S(1)}, u32[]{:S(2)}, u32[]{:S(2)}) collective-permute-start(bf16[1,1,1,1,1,24,1536]{6,5,4,3,2,1,0:T(8,128)(2,1)S(1)} %constant_dynamic-slice_fusion.3), channel_id=1, source_target_pairs={{0,4},{1,5},{2,6},{3,7},{4,0},{5,1},{6,2},{7,3},{8,12},{9,13},{10,... | collective-permute-start | bytes 221192 | tf_op jit(solution)/shard_map/ppermute | solution.py:620
  646.5 6.6 collective-permute-start.18
  646.5 110.2 %all-to-all-start.5 = ((bf16[256,16,384]{2,1,0:T(8,128)(2,1)}), bf16[256,16,384]{2,1,0:T(8,128)(2,1)}, u32[]{:S(2)}, u32[]{:S(2)}) async-start(bf16[256,16,384]{2,1,0:T(8,128)(2,1)} %bitcast.60), calls=%async_computation.5 | async-start | bytes 6291456 | tf_op jit(solution)/shard_map/all_to_all | solution.py:628
  656.7 40.7 %collective-permute-start.19 = (bf16[1,1,18,2,64,384]{5,4,3,2,1,0:T(8,128)(2,1)S(1)}, bf16[1,1,18,2,64,384]{5,4,3,2,1,0:T(8,128)(2,1)S(1)}, u32[]{:S(2)}, u32[]{:S(2)}) collective-permute-start(bf16[1,1,18,2,64,384]{5,4,3,2,1,0:T(8,128)(2,1)S(1)} %constant_dynamic-slice_fusion), channel_id=1, source_target_pairs={{0,16},{8,24},{16,0},{24,8},{1,17},{9,25},{17,1},{25,9},{2,18},{10... | collective-permute-start | bytes 5308424 | tf_op jit(solution)/shard_map/ppermute | solution.py:620
  698.3 69.8 %copy-start = (bf16[16,2,64,384]{3,2,1,0:T(8,128)(2,1)}, bf16[16,2,64,384]{3,2,1,0:T(8,128)(2,1)S(1)}, u32[]{:S(2)}) copy-start(bf16[16,2,64,384]{3,2,1,0:T(8,128)(2,1)S(1)} %slice_bitcast_fusion.refs_3_.rest_0_) | copy-start | bytes 4718596
  698.3 35.8 %collective-permute-start.23 = (bf16[16,2,64,384]{3,2,1,0:T(8,128)(2,1)S(1)}, bf16[16,2,64,384]{3,2,1,0:T(8,128)(2,1)S(1)}, u32[]{:S(2)}, u32[]{:S(2)}) collective-permute-start(bf16[16,2,64,384]{3,2,1,0:T(8,128)(2,1)S(1)} %slice_bitcast_fusion.refs_3_.rest_0_), channel_id=1, source_target_pairs={{0,16},{8,24},{16,0},{24,8},{1,17},{9,25},{17,1},{25,9},{2,18},{10... | collective-permute-start | bytes 4718600 | tf_op jit(solution)/shard_map/ppermute | solution.py:620
  699.8 68.3 %collective-permute-start.20 = (bf16[16,2,64,384]{3,2,1,0:T(8,128)(2,1)S(1)}, bf16[16,2,64,384]{3,2,1,0:T(8,128)(2,1)}, u32[]{:S(2)}, u32[]{:S(2)}) collective-permute-start(bf16[16,2,64,384]{3,2,1,0:T(8,128)(2,1)S(1)} %slice_bitcast_fusion.refs_3_.rest_0_), channel_id=1, source_target_pairs={{0,7},{1,6},{2,5},{3,4},{4,3},{5,2},{6,1},{7,0},{8,15},{9,14},{10,... | collective-permute-start | bytes 4718600 | tf_op jit(solution)/shard_map/ppermute | solution.py:620
  702.5 65.7 %collective-permute-start.22 = (bf16[16,2,64,384]{3,2,1,0:T(8,128)(2,1)S(1)}, bf16[16,2,64,384]{3,2,1,0:T(8,128)(2,1)}, u32[]{:S(2)}, u32[]{:S(2)}) collective-permute-start(bf16[16,2,64,384]{3,2,1,0:T(8,128)(2,1)S(1)} %slice_bitcast_fusion.refs_3_.rest_0_), channel_id=1, source_target_pairs={{0,8},{8,0},{16,24},{24,16},{1,9},{9,1},{17,25},{25,17},{2,10},{10... | collective-permute-start | bytes 4718600 | tf_op jit(solution)/shard_map/ppermute | solution.py:620
  734.1 34.1 %copy-start.2 = (bf16[16,2,64,384]{3,2,1,0:T(8,128)(2,1)}, bf16[16,2,64,384]{3,2,1,0:T(8,128)(2,1)S(1)}, u32[]{:S(2)}) copy-start(bf16[16,2,64,384]{3,2,1,0:T(8,128)(2,1)S(1)} %collective-permute-done.23.refs_5_.rest_2_) | copy-start | bytes 4718596
  734.1 34.1 %collective-permute-start.24 = (bf16[16,2,64,384]{3,2,1,0:T(8,128)(2,1)S(1)}, bf16[16,2,64,384]{3,2,1,0:T(8,128)(2,1)}, u32[]{:S(2)}, u32[]{:S(2)}) collective-permute-start(bf16[16,2,64,384]{3,2,1,0:T(8,128)(2,1)S(1)} %collective-permute-done.23.refs_5_.rest_2_), channel_id=1, source_target_pairs={{0,8},{8,0},{16,24},{24,16},{1,9},{9,1},{17,25},{25,17},{2,10},{10... | collective-permute-start | bytes 4718600 | tf_op jit(solution)/shard_map/ppermute | solution.py:620
  734.1 34.0 %collective-permute-start.21 = (bf16[2,64,384]{2,1,0:T(8,128)(2,1)S(1)}, bf16[2,64,384]{2,1,0:T(8,128)(2,1)S(1)}, u32[]{:S(2)}, u32[]{:S(2)}) collective-permute-start(bf16[2,64,384]{2,1,0:T(8,128)(2,1)S(1)} %fusion.1), channel_id=1, source_target_pairs={{0,4},{1,7},{2,6},{3,5},{8,12},{9,15},{10,14},{11,13},{16,20},{17,... | collective-permute-start | bytes 294920 | tf_op jit(solution)/shard_map/ppermute | solution.py:744
  768.1 0.6 copy-start.8
  768.8 30.5 %copy-start.9 = (bf16[2,64,384]{2,1,0:T(8,128)(2,1)S(1)}, bf16[2,64,384]{2,1,0:T(8,128)(2,1)}, u32[]{:S(2)}) copy-start(bf16[2,64,384]{2,1,0:T(8,128)(2,1)} %copy-done.8) | copy-start | bytes 294916
  768.8 150.1 %all-to-all-start.6 = ((bf16[256,16,384]{2,1,0:T(8,128)(2,1)}), bf16[256,16,384]{2,1,0:T(8,128)(2,1)S(1)}, u32[]{:S(2)}, u32[]{:S(2)}) async-start(bf16[256,16,384]{2,1,0:T(8,128)(2,1)} %hold.3), calls=%async_computation.6 | async-start | bytes 6291456 | tf_op jit(solution)/shard_map/all_to_all | solution.py:628
  798.5 42.6 %copy-start.15 = (f32[2,384]{1,0:T(2,128)S(1)}, f32[2,384]{1,0:T(2,128)}, u32[]{:S(2)}) copy-start(f32[2,384]{1,0:T(2,128)} %add_multiply_fusion.rest_4_) | copy-start | bytes 9220
  798.5 96.4 %all-gather.3.cloned.1.call-start = ((), (), s32[]{:S(2)}) async-start(), calls=%async_computation.7 | async-start | bytes 2433024 | tf_op jit(solution)/shard_map/all_gather | solution.py:734
  802.1 39.0 %collective-permute-start.26 = (bf16[17,2,64,384]{3,2,1,0:T(8,128)(2,1)}, bf16[17,2,64,384]{3,2,1,0:T(8,128)(2,1)}, u32[]{:S(2)}, u32[]{:S(2)}) collective-permute-start(bf16[17,2,64,384]{3,2,1,0:T(8,128)(2,1)} %pad_maximum_fusion.1.rest_4_), channel_id=1, source_target_pairs={{0,16},{8,24},{16,0},{24,8},{1,17},{9,25},{17,1},{25,9},{2,18},{10... | collective-permute-start | bytes 5013512 | tf_op jit(solution)/shard_map/ppermute | solution.py:620
  803.5 97.0 %collective-permute-start.25 = (bf16[17,2,64,384]{3,2,1,0:T(8,128)(2,1)}, bf16[17,2,64,384]{3,2,1,0:T(8,128)(2,1)}, u32[]{:S(2)}, u32[]{:S(2)}) collective-permute-start(bf16[17,2,64,384]{3,2,1,0:T(8,128)(2,1)} %pad_maximum_fusion.1.rest_4_), channel_id=1, source_target_pairs={{0,8},{8,0},{16,24},{24,16},{1,9},{9,1},{17,25},{25,17},{2,10},{10... | collective-permute-start | bytes 5013512 | tf_op jit(solution)/shard_map/ppermute | solution.py:620
  841.1 59.4 %collective-permute-start.27 = (bf16[17,2,64,384]{3,2,1,0:T(8,128)(2,1)}, bf16[17,2,64,384]{3,2,1,0:T(8,128)(2,1)}, u32[]{:S(2)}, u32[]{:S(2)}) collective-permute-start(bf16[17,2,64,384]{3,2,1,0:T(8,128)(2,1)} %collective-permute-done.26.rest_6_), channel_id=1, source_target_pairs={{0,8},{8,0},{16,24},{24,16},{1,9},{9,1},{17,25},{25,17},{2,10},{10... | collective-permute-start | bytes 5013512 | tf_op jit(solution)/shard_map/ppermute | solution.py:620
  918.9 1.6 copy-start.1
Sparse Core Ops, SparseCore 0:
  802.9 92.0 all-gather.2

commit v2 on v1

--- a/solution.py
+++ b/solution.py
@@ -628,6 +628,10 @@
     return lax.all_to_all(value, "space", split_axis=0, concat_axis=0, tiled=True)
 
 
+def exchange_after(value, after):
+    return exchange(hold(value, tuple(after)) if after else value)
+
+
 def gather_copies(value, copies):
     parts = {0: value}
     bit = copies // 2
@@ -708,14 +712,15 @@
     returned, spectrum = columns(flags(copy), (forward_in, out_tabs), kernel, arrived, chunks)
 
     tables = (table_out, table_in)
-    arrived = []
+    received, arrived = [], []
+    for r in returned:
+        received.append(exchange_after(join(r), received))
     previous = None
     for c in range(chunks):
-        received = exchange(join(returned[c]))
         block_out, sent, sums = mlp(
-            [received], tokens, upstream, gain_b, tables, weights, previous, c, 4
+            [received[c]], tokens, upstream, gain_b, tables, weights, previous, c, 4
         )
-        arrived.append(split(exchange(sent[0])))
+        arrived.append(exchange_after(sent[0], arrived))
         previous = [block_out, *sums]
 
     axes = ("copy", "space")
@@ -729,11 +734,13 @@
     gains = gains * factor
 
     returned, terms = columns(
-        flags(copy), (backward_in, out_tabs), kernel, arrived, chunks, spectrum, (part, gains)
+        flags(copy), (backward_in, out_tabs), kernel, [split(a) for a in arrived], chunks, spectrum, (part, gains)
     )
     grads = lax.all_gather(part, axes, tiled=True)
     received = exchange(join(returned[0]))
-    grad_tokens = leave([received], tokens, upstream, gain_a, table_out, None, 0, 2, ())
+    grad_tokens = leave(
+        [received], tokens, upstream, gain_a, table_out, None, 0, 2, (grads,)
+    )
 
     terms = terms.reshape(terms.shape[:2] + digits + (share, chans))
     terms = jnp.moveaxis(terms, range(2, 2 + len(digits)), range(len(digits)))

time: 946 us -> 851 us (0.90)
  waiting for transfers between devices: 472 us -> 376 us
    all_to_all x6, waiting for transfers between devices: 169 us -> 87.9 us  [exchange(): lax.all_to_all(value, 'space', split_axis=0, concat_axis=0, tiled=True)]
    all_to_all x6, starting transfers between devices: 51.8 us -> 34.7 us  [exchange(): lax.all_to_all(value, 'space', split_axis=0, concat_axis=0, tiled=True)]
    ppermute x26, starting transfers between devices: 31.9 us -> 44.6 us  [swap(): return lax.ppermute(value, axis, [(i, partner(i)) for i in range(size)])]
    unnamed x41 -> x51, local copies, waits for them, and re-layouts: 16.1 us -> 20.1 us
  transfers between devices with their start and end apart: 35 -> 35, of which waited for: 20 -> 19; matrix products, arithmetic and copies ran while one was open for 3% -> 3% of each run, Pallas kernels for 14% -> 24%
where the time goes in v2:
time: 851 us; the launch traced here: 844 us
  waiting for transfers between devices  376 us (44%)
  Pallas kernels  248 us (29%)
  starting transfers between devices  83.4 us (10%)
  blocking collectives  74.7 us (9%)
  local copies, waits for them, and re-layouts  32.1 us (4%)
  other arithmetic  15.1 us (2%)
  between operations  14.7 us (2%)
    ppermute x26, waiting for transfers between devices, swap(): return lax.ppermute(value, axis, [(i, partner(i)) for i in range(size)])  193 us
    pallas_call x2, Pallas kernels, mlp(): pl.pallas_call(functools.partial(mlp_kernel, n, previous is not None), gr...  135 us
    all_to_all x6, waiting for transfers between devices, exchange(): lax.all_to_all(value, 'space', split_axis=0, concat_axis=0, tiled=True)  87.9 us
    all_to_all x1, blocking collectives, exchange(): lax.all_to_all(value, 'space', split_axis=0, concat_axis=0, tiled=True)  74.7 us
    ppermute x1, waiting for transfers between devices, body(): single = lax.ppermute(single.reshape(2, share, chans), 'space', to_lower)  49.3 us
    all_gather x1, waiting for transfers between devices, body(): grads = lax.all_gather(part, axes, tiled=True)  45.6 us
    ppermute x26, starting transfers between devices, swap(): return lax.ppermute(value, axis, [(i, partner(i)) for i in range(size)])  44.6 us
    pallas_call x2, Pallas kernels, columns(): pl.pallas_call(functools.partial(columns_kernel, count, outs, back), grid...  37.8 us
  transfers between devices with their start and end apart: 35, of which 19 were waited for; matrix products, arithmetic and copies ran while one was open for 3% of the time, Pallas kernels for 24%

profile of v2, /device:TPU:0, one launch (start us, length us, event | category | flops | bytes accessed | tf_op | source)
XLA Modules:
  0.0 844.1 jit_solution(187146797658035866)
XLA Ops:
  7.2 1.6 constant_dynamic-slice_fusion.9
  8.8 6.1 collective-permute-start
  14.8 1.3 constant_dynamic-slice_fusion.8
  16.1 1.3 collective-permute-start.4
  18.0 19.0 %enter_rows.1.refs_0_ = bf16[256,32,384]{2,1,0:T(8,128)(2,1)} custom-call(bf16[32,256,384]{2,1,0:T(8,128)(2,1)} %bitcast.41, f32[1,384]{1,0:T(1,128)} %reshape.65.gain, bf16[256,256]{1,0:T(8,128)(2,1)} %constant.87.clone.table.table_in), custom_call_target="tpu_custom_call" | custom-call | flops 1610612736 | bytes 12582912 | tf_op jit(solution)/shard_map/enter_rows/pallas_call | solution.py:208
  37.0 49.3 %collective-permute-done.4.rest_4_.refs_2_ = bf16[2,64,384]{2,1,0:T(8,128)(2,1)S(1)} collective-permute-done((bf16[2,64,384]{2,1,0:T(8,128)(2,1)S(1)}, bf16[2,64,384]{2,1,0:T(8,128)(2,1)S(1)}, u32[]{:S(2)}, u32[]{:S(2)}) %collective-permute-start.4) | collective-permute-done | bytes 98336 | tf_op jit(solution)/shard_map/ppermute | solution.py:681
  88.1 5.0 all-to-all-start
  93.1 1.6 collective-permute-start.2
  94.6 34.0 %collective-permute-done.2.rest_2_ = bf16[2,64,16,384]{3,2,1,0:T(8,128)(2,1)S(1)} collective-permute-done((bf16[2,64,16,384]{3,2,1,0:T(8,128)(2,1)S(1)}, bf16[2,64,16,384]{3,2,1,0:T(8,128)(2,1)S(1)}, u32[]{:S(2)}, u32[]{:S(2)}) %collective-permute-start.2) | collective-permute-done | bytes 1572896 | tf_op jit(solution)/shard_map/ppermute | solution.py:620
  128.7 1.6 collective-permute-start.6
  130.2 2.4 copy.29
  132.6 2.4 copy.30
  137.1 15.4 %filter_part.1.kernel = bf16[18,2,256,384]{3,2,1,0:T(8,128)(2,1)} custom-call(s32[3]{0:T(128)} %pad_add_fusion.flags, bf16[256,256]{1,0:T(8,128)(2,1)} %constant.92.clone.mirror, bf16[2,256,32,384]{3,2,1,0:T(8,128)(2,1)} %own.1, bf16[2,64,16,384]{3,2,1,0:T(8,128)(2,1)} %copy-done.8, bf16[2,64,16,384]{3,2,1,0:T(8,128)(2,1)} %collective-permute-done.1.rest_1_, ...), custom_call_target="tpu_custom_call" | custom-call | flops 1610612736 | bytes 25165824 | tf_op jit(solution)/shard_map/filter_part/pallas_call | solution.py:521
  152.5 78.4 %all-to-all-done = bf16[256,32,384]{2,1,0:T(8,128)(2,1)} async-done(((bf16[256,32,384]{2,1,0:T(8,128)(2,1)}), bf16[256,32,384]{2,1,0:T(8,128)(2,1)}, u32[]{:S(2)}, u32[]{:S(2)}) %all-to-all-start) | async-done | bytes 6291488 | tf_op jit(solution)/shard_map/all_to_all | solution.py:628
  230.8 18.1 %filter_columns.2 = (bf16[8,2,16,16,384]{4,3,2,1,0:T(8,128)(2,1)}, bf16[8,2,16,16,384]{4,3,2,1,0:T(8,128)(2,1)}, bf16[18,2,256,384]{3,2,1,0:T(8,128)(2,1)}) custom-call(s32[3]{0:T(128)} %pad_add_fusion.flags, bf16[3,512,512]{2,1,0:T(8,128)(2,1)} %constant.89.clone.table_f, bf16[3,512,512]{2,1,0:T(8,128)(2,1)} %constant.91.clone.table_b, ...), custom_call_target="tpu_custom_call" | custom-call | flops 7247757312 | bytes 35389440 | tf_op jit(solution)/shard_map/filter_columns/pallas_call | solution.py:444
  249.0 74.7 %all_to_all.35.refs_1_.rest_0_ = bf16[256,16,384]{2,1,0:T(8,128)(2,1)} all-to-all(bf16[256,16,384]{2,1,0:T(8,128)(2,1)} %bitcast.65), channel_id=1, replica_groups=mesh['copy'=4,'space'=8] {'space'}, dimensions={0} | all-to-all | bytes 6291456 | tf_op jit(solution)/shard_map/all_to_all | solution.py:628
  323.7 3.8 all-to-all-start.2
  328.1 66.5 %mlp_rows.2 = (bf16[32,256,384]{2,1,0:T(8,128)(2,1)}, bf16[256,16,384]{2,1,0:T(8,128)(2,1)}, f32[384,1536]{1,0:T(8,128)}, f32[384,1536]{1,0:T(8,128)}, f32[16,384]{1,0:T(8,128)}) custom-call(bf16[32,256,384]{2,1,0:T(8,128)(2,1)} %bitcast.42, bf16[32,256,384]{2,1,0:T(8,128)(2,1)} %bitcast.47, f32[1,384]{1,0:T(1,128)} %reshape.63.gain, ...), custom_call_target="tpu_custom_call" | custom-call | flops 30601641984 | bytes 15728640 | tf_op jit(solution)/shard_map/mlp_rows/pallas_call | solution.py:313
  394.6 3.0 all-to-all-done.2.rest_0_
  397.5 1.7 copy-done.10
  399.2 3.6 all-to-all-start.3
  402.9 68.2 %mlp_rows.3 = (bf16[32,256,384]{2,1,0:T(8,128)(2,1)}, bf16[256,16,384]{2,1,0:T(8,128)(2,1)}, f32[384,1536]{1,0:T(8,128)}, f32[384,1536]{1,0:T(8,128)}, f32[16,384]{1,0:T(8,128)}) custom-call(bf16[32,256,384]{2,1,0:T(8,128)(2,1)} %bitcast.43, bf16[32,256,384]{2,1,0:T(8,128)(2,1)} %bitcast.48, ...), custom_call_target="tpu_custom_call", output_to_operand_aliasing={{0}: (10, {})} | custom-call | flops 30601641984 | bytes 15728640 | tf_op jit(solution)/shard_map/mlp_rows/pallas_call | solution.py:313
  471.1 1.9 convert.10
  475.6 1.7 copy-done.3
  477.3 6.1 all-to-all-start.4
  483.4 1.6 add_convert_fusion.1
  485.1 1.5 collective-permute-start.9
  487.4 13.2 %collective-permute-done.9 = bf16[1,1,2,2,2,24,1536]{6,5,4,3,2,1,0:T(8,128)(2,1)S(1)} collective-permute-done((bf16[1,1,2,2,2,24,1536]{6,5,4,3,2,1,0:T(8,128)(2,1)S(1)}, bf16[1,1,2,2,2,24,1536]{6,5,4,3,2,1,0:T(8,128)(2,1)S(1)}, u32[]{:S(2)}, u32[]{:S(2)}) %collective-permute-start.9) | collective-permute-done | bytes 589856 | tf_op jit(solution)/shard_map/ppermute | solution.py:620
  500.8 1.8 collective-permute-start.10
  503.8 1.5 collective-permute-start.14
  505.3 11.5 %collective-permute-done.10 = bf16[1,1,2,2,1,24,1536]{6,5,4,3,2,1,0:T(8,128)(2,1)S(1)} collective-permute-done((bf16[1,1,2,2,1,24,1536]{6,5,4,3,2,1,0:T(8,128)(2,1)S(1)}, bf16[1,1,2,2,1,24,1536]{6,5,4,3,2,1,0:T(8,128)(2,1)S(1)}, u32[]{:S(2)}, u32[]{:S(2)}) %collective-permute-start.10) | collective-permute-done | bytes 294944 | tf_op jit(solution)/shard_map/ppermute | solution.py:620
  517.7 2.6 collective-permute-start.15
  520.3 1.6 collective-permute-done.15
  521.9 1.6 collective-permute-start.16
  523.5 15.8 %collective-permute-done.16 = f32[2,384]{1,0:T(2,128)S(1)} collective-permute-done((f32[2,384]{1,0:T(2,128)S(1)}, f32[2,384]{1,0:T(2,128)S(1)}, u32[]{:S(2)}, u32[]{:S(2)}) %collective-permute-start.16) | collective-permute-done | bytes 3104 | tf_op jit(solution)/shard_map/ppermute | solution.py:620
  539.3 18.0 %collective-permute-start.17 = (f32[2,384]{1,0:T(2,128)S(1)}, f32[2,384]{1,0:T(2,128)S(1)}, u32[]{:S(2)}, u32[]{:S(2)}) collective-permute-start(f32[2,384]{1,0:T(2,128)S(1)} %add.105), channel_id=1, source_target_pairs={{0,4},{1,5},{2,6},{3,7},{4,0},{5,1},{6,2},{7,3},{8,12},{9,13},{10,... | collective-permute-start | bytes 9224 | tf_op jit(solution)/shard_map/ppermute | solution.py:620
  557.5 1.4 collective-permute-done.17
  559.5 3.6 collective-permute-done.12
  563.7 19.7 %filter_columns.3 = (bf16[8,2,16,16,384]{4,3,2,1,0:T(8,128)(2,1)}, bf16[8,2,16,16,384]{4,3,2,1,0:T(8,128)(2,1)}, bf16[18,2,256,384]{3,2,1,0:T(8,128)(2,1)}) custom-call(s32[3]{0:T(128)} %pad_add_fusion.flags, bf16[3,512,512]{2,1,0:T(8,128)(2,1)} %constant.90.clone.table_f, bf16[3,512,512]{2,1,0:T(8,128)(2,1)} %constant.91.clone.table_b, ...), custom_call_target="tpu_custom_call" | custom-call | flops 7247757312 | bytes 35389440 | tf_op jit(solution)/shard_map/filter_columns/pallas_call | solution.py:444
  583.4 4.1 constant_dynamic-slice_fusion.2
  587.5 2.2 copy.41
  589.7 4.5 all-to-all-start.5
  594.2 2.0 collective-permute-done.18
  596.3 3.3 fusion
  599.6 1.8 copy-done.1
  601.6 1.5 collective-permute-start.19
  603.2 39.7 %collective-permute-done.19 = bf16[1,1,18,2,64,384]{5,4,3,2,1,0:T(8,128)(2,1)S(1)} collective-permute-done((bf16[1,1,18,2,64,384]{5,4,3,2,1,0:T(8,128)(2,1)S(1)}, bf16[1,1,18,2,64,384]{5,4,3,2,1,0:T(8,128)(2,1)S(1)}, u32[]{:S(2)}, u32[]{:S(2)}) %collective-permute-start.19) | collective-permute-done | bytes 1769504 | tf_op jit(solution)/shard_map/ppermute | solution.py:620
  642.9 2.1 add_convert_fusion
  645.2 2.5 collective-permute-start.23
  647.7 1.6 collective-permute-start.20
  649.3 31.6 %collective-permute-done.23.refs_5_.rest_2_ = bf16[16,2,64,384]{3,2,1,0:T(8,128)(2,1)S(1)} collective-permute-done((bf16[16,2,64,384]{3,2,1,0:T(8,128)(2,1)S(1)}, bf16[16,2,64,384]{3,2,1,0:T(8,128)(2,1)S(1)}, u32[]{:S(2)}, u32[]{:S(2)}) %collective-permute-start.23) | collective-permute-done | bytes 1572896 | tf_op jit(solution)/shard_map/ppermute | solution.py:620
  681.0 2.8 collective-permute-start.21
  683.8 45.6 %all-gather.3.cloned.1.call-done = bf16[1,1,1,1,1,768,1536]{6,5,4,3,2,1,0:T(8,128)(2,1)} async-done(((bf16[1,1,1,1,1,24,1536]{6,5,4,3,2,1,0:T(8,128)(2,1)}), bf16[1,1,1,1,1,768,1536]{6,5,4,3,2,1,0:T(8,128)(2,1)}) %all-gather.3.cloned.1.call-update) | async-done | bytes 2359312 | tf_op jit(solution)/shard_map/all_gather | solution.py:739
  729.3 11.4 %leave_rows.2.refs_7_.rest_1_ = bf16[32,256,384]{2,1,0:T(8,128)(2,1)} custom-call(bf16[32,256,384]{2,1,0:T(8,128)(2,1)} %bitcast.44, bf16[32,256,384]{2,1,0:T(8,128)(2,1)} %bitcast.49, f32[1,384]{1,0:T(1,128)} %reshape.65.gain, bf16[256,256]{1,0:T(8,128)(2,1)} %constant.88.clone.table_out, bf16[256,16,384]{2,1,0:T(8,128)(2,1)} %all-to-all-done.5.rest_0_, ...), custom_call_target="tpu_custom_call" | custom-call | flops 805306368 | bytes 12582912 | tf_op jit(solution)/shard_map/leave_rows/pallas_call | solution.py:369
  741.4 11.7 %all-to-all-start.6 = ((bf16[256,16,384]{2,1,0:T(8,128)(2,1)}), bf16[256,16,384]{2,1,0:T(8,128)(2,1)S(1)}, u32[]{:S(2)}, u32[]{:S(2)}) async-start(bf16[256,16,384]{2,1,0:T(8,128)(2,1)} %hold.7), calls=%async_computation.6 | async-start | bytes 6291456 | tf_op jit(solution)/shard_map/all_to_all | solution.py:628
  753.2 2.9 pad_maximum_fusion.1.rest_4_
  756.1 1.4 collective-permute-start.26
  757.5 37.1 %collective-permute-done.26.rest_6_ = bf16[17,2,64,384]{3,2,1,0:T(8,128)(2,1)} collective-permute-done((bf16[17,2,64,384]{3,2,1,0:T(8,128)(2,1)}, bf16[17,2,64,384]{3,2,1,0:T(8,128)(2,1)}, u32[]{:S(2)}, u32[]{:S(2)}) %collective-permute-start.26) | collective-permute-done | bytes 1671200 | tf_op jit(solution)/shard_map/ppermute | solution.py:620
  795.2 1.6 slice_bitcast_fusion.1
  796.8 2.4 copy.34
  799.2 18.3 %filter_gradient.1.rest_2_ = f32[2,256,32,384]{3,2,1,0:T(8,128)} custom-call(s32[3]{0:T(128)} %pad_add_fusion.flags, bf16[256,256]{1,0:T(8,128)(2,1)} %constant.92.clone.mirror, bf16[16,2,64,384]{3,2,1,0:T(8,128)(2,1)} %copy-done, bf16[16,2,64,384]{3,2,1,0:T(8,128)(2,1)} %collective-permute-done.22.refs_4_.rest_1_, bf16[16,2,64,384]{3,2,1,0:T(8,128)(2,1)} %copy-done.7, ...), custom_call_target="tpu_custom_call" | custom-call | flops 1610612736 | bytes 37748736 | tf_op jit(solution)/shard_map/filter_gradient/pallas_call | solution.py:597
  817.5 6.5 all-to-all-done.6.rest_0_
  824.0 1.6 copy-done.2
  825.7 11.4 %leave_rows.3 = bf16[32,256,384]{2,1,0:T(8,128)(2,1)} custom-call(bf16[32,256,384]{2,1,0:T(8,128)(2,1)} %bitcast.45, bf16[32,256,384]{2,1,0:T(8,128)(2,1)} %bitcast.50, f32[1,384]{1,0:T(1,128)} %reshape.65.gain, bf16[256,256]{1,0:T(8,128)(2,1)} %constant.88.clone.table_out, bf16[256,16,384]{2,1,0:T(8,128)(2,1)} %copy-done.2, ...), custom_call_target="tpu_custom_call", output_to_operand_aliasing={{}: (5, {})} | custom-call | flops 805306368 | bytes 12582912 | tf_op jit(solution)/shard_map/leave_rows/pallas_call | solution.py:369
  (109 shorter events, 13.8 us)
Async XLA Ops:
  7.2 10.3 %copy-start.21 = (f32[384]{0:T(512)S(1)}, f32[384]{0:T(512)}, u32[]{:S(2)}) copy-start(f32[384]{0:T(512)} %param.18) | copy-start | bytes 4612
  8.8 77.5 %collective-permute-start = (bf16[2,64,16,384]{3,2,1,0:T(8,128)(2,1)S(1)}, bf16[2,64,16,384]{3,2,1,0:T(8,128)(2,1)S(1)}, u32[]{:S(2)}, u32[]{:S(2)}) collective-permute-start(bf16[2,64,16,384]{3,2,1,0:T(8,128)(2,1)S(1)} %constant_dynamic-slice_fusion.9), channel_id=1, source_target_pairs={{0,7},{1,6},{2,5},{3,4},{4,3},{5,2},{6,1},{7,0},{8,15},{9,14},{10,... | collective-permute-start | bytes 4718600 | tf_op jit(solution)/shard_map/ppermute | solution.py:620
  16.1 70.2 %collective-permute-start.4 = (bf16[2,64,384]{2,1,0:T(8,128)(2,1)S(1)}, bf16[2,64,384]{2,1,0:T(8,128)(2,1)S(1)}, u32[]{:S(2)}, u32[]{:S(2)}) collective-permute-start(bf16[2,64,384]{2,1,0:T(8,128)(2,1)S(1)} %bitcast.68), channel_id=1, source_target_pairs={{4,0},{5,3},{6,2},{7,1},{12,8},{13,11},{14,10},{15,9},{20,16},{21,... | collective-permute-start | bytes 294920 | tf_op jit(solution)/shard_map/ppermute | solution.py:681
  86.3 0.6 copy-start.15
  87.0 1.1 copy-start.8
  88.1 5.0 copy-start.9
  88.1 40.6 %copy-start.16 = (bf16[2,64,384]{2,1,0:T(8,128)(2,1)S(1)}, bf16[2,64,384]{2,1,0:T(8,128)(2,1)}, u32[]{:S(2)}) copy-start(bf16[2,64,384]{2,1,0:T(8,128)(2,1)} %copy-done.15) | copy-start | bytes 294916
  88.1 142.7 %all-to-all-start = ((bf16[256,32,384]{2,1,0:T(8,128)(2,1)}), bf16[256,32,384]{2,1,0:T(8,128)(2,1)}, u32[]{:S(2)}, u32[]{:S(2)}) async-start(bf16[256,32,384]{2,1,0:T(8,128)(2,1)} %hold.4), calls=%async_computation | async-start | bytes 12582912 | tf_op jit(solution)/shard_map/all_to_all | solution.py:628
  93.1 35.6 %collective-permute-start.2 = (bf16[2,64,16,384]{3,2,1,0:T(8,128)(2,1)S(1)}, bf16[2,64,16,384]{3,2,1,0:T(8,128)(2,1)S(1)}, u32[]{:S(2)}, u32[]{:S(2)}) collective-permute-start(bf16[2,64,16,384]{3,2,1,0:T(8,128)(2,1)S(1)} %copy-done.9), channel_id=1, source_target_pairs={{0,16},{8,24},{16,0},{24,8},{1,17},{9,25},{17,1},{25,9},{2,18},{10... | collective-permute-start | bytes 4718600 | tf_op jit(solution)/shard_map/ppermute | solution.py:620
  94.6 41.8 %collective-permute-start.1 = (bf16[2,64,16,384]{3,2,1,0:T(8,128)(2,1)S(1)}, bf16[2,64,16,384]{3,2,1,0:T(8,128)(2,1)}, u32[]{:S(2)}, u32[]{:S(2)}) collective-permute-start(bf16[2,64,16,384]{3,2,1,0:T(8,128)(2,1)S(1)} %copy-done.9), channel_id=1, source_target_pairs={{0,8},{8,0},{16,24},{24,16},{1,9},{9,1},{17,25},{25,17},{2,10},{10... | collective-permute-start | bytes 4718600 | tf_op jit(solution)/shard_map/ppermute | solution.py:620
  128.7 6.3 copy-start.12
  128.7 7.8 collective-permute-start.3
  128.7 6.5 collective-permute-start.6
  135.0 1.3 collective-permute-start.5
  135.1 1.3 copy-start.17
  135.1 1.3 collective-permute-start.7
  136.3 0.7 copy-start.18
  136.4 0.7 copy-start.19
  323.7 3.8 copy-start.22
  323.7 73.8 %all-to-all-start.2 = ((bf16[256,16,384]{2,1,0:T(8,128)(2,1)}), bf16[256,16,384]{2,1,0:T(8,128)(2,1)S(1)}, u32[]{:S(2)}, u32[]{:S(2)}) async-start(bf16[256,16,384]{2,1,0:T(8,128)(2,1)} %hold.5), calls=%async_computation.2 | async-start | bytes 6291456 | tf_op jit(solution)/shard_map/all_to_all | solution.py:628
  397.5 1.7 copy-start.10
  399.2 76.4 %all-to-all-start.3 = ((bf16[256,16,384]{2,1,0:T(8,128)(2,1)}), bf16[256,16,384]{2,1,0:T(8,128)(2,1)S(1)}, u32[]{:S(2)}, u32[]{:S(2)}) async-start(bf16[256,16,384]{2,1,0:T(8,128)(2,1)} %get-tuple-element.31), calls=%async_computation.3 | async-start | bytes 6291456 | tf_op jit(solution)/shard_map/all_to_all | solution.py:628
  471.1 2.4 copy-start.11
  473.8 1.8 copy-start.4
  475.6 7.8 collective-permute-start.8
  475.6 1.7 copy-start.3
  477.3 6.1 copy-start.5
  477.3 86.5 %all-to-all-start.4 = ((bf16[256,16,384]{2,1,0:T(8,128)(2,1)}), bf16[256,16,384]{2,1,0:T(8,128)(2,1)}, u32[]{:S(2)}, u32[]{:S(2)}) async-start(bf16[256,16,384]{2,1,0:T(8,128)(2,1)} %hold.6), calls=%async_computation.4 | async-start | bytes 6291456 | tf_op jit(solution)/shard_map/all_to_all | solution.py:628
  485.1 15.5 %collective-permute-start.9 = (bf16[1,1,2,2,2,24,1536]{6,5,4,3,2,1,0:T(8,128)(2,1)S(1)}, bf16[1,1,2,2,2,24,1536]{6,5,4,3,2,1,0:T(8,128)(2,1)S(1)}, u32[]{:S(2)}, u32[]{:S(2)}) collective-permute-start(bf16[1,1,2,2,2,24,1536]{6,5,4,3,2,1,0:T(8,128)(2,1)S(1)} %constant_dynamic-slice_fusion.6), channel_id=1, source_target_pairs={{0,16},{8,24},{16,0},{24,8},{1,17},{9,25},{17,1},{25,9},{2,18},{10... | collective-permute-start | bytes 1769480 | tf_op jit(solution)/shard_map/ppermute | solution.py:620
  500.8 16.1 %collective-permute-start.10 = (bf16[1,1,2,2,1,24,1536]{6,5,4,3,2,1,0:T(8,128)(2,1)S(1)}, bf16[1,1,2,2,1,24,1536]{6,5,4,3,2,1,0:T(8,128)(2,1)S(1)}, u32[]{:S(2)}, u32[]{:S(2)}) collective-permute-start(bf16[1,1,2,2,1,24,1536]{6,5,4,3,2,1,0:T(8,128)(2,1)S(1)} %constant_dynamic-slice_fusion.5), channel_id=1, source_target_pairs={{0,1},{1,0},{2,3},{3,2},{4,5},{5,4},{6,7},{7,6},{8,9},{9,8},{10,11... | collective-permute-start | bytes 884744 | tf_op jit(solution)/shard_map/ppermute | solution.py:620
  502.6 1.2 collective-permute-start.13
  503.8 13.9 %collective-permute-start.14 = (f32[2,384]{1,0:T(2,128)S(1)}, f32[2,384]{1,0:T(2,128)S(1)}, u32[]{:S(2)}, u32[]{:S(2)}) collective-permute-start(f32[2,384]{1,0:T(2,128)S(1)} %fusion.2), channel_id=1, source_target_pairs={{0,16},{8,24},{16,0},{24,8},{1,17},{9,25},{17,1},{25,9},{2,18},{10... | collective-permute-start | bytes 9224 | tf_op jit(solution)/shard_map/ppermute | solution.py:620
  517.0 40.3 %collective-permute-start.11 = (bf16[1,1,2,1,1,24,1536]{6,5,4,3,2,1,0:T(8,128)(2,1)S(1)}, bf16[1,1,2,1,1,24,1536]{6,5,4,3,2,1,0:T(8,128)(2,1)S(1)}, u32[]{:S(2)}, u32[]{:S(2)}) collective-permute-start(bf16[1,1,2,1,1,24,1536]{6,5,4,3,2,1,0:T(8,128)(2,1)S(1)} %constant_dynamic-slice_fusion.4), channel_id=1, source_target_pairs={{0,2},{1,3},{2,0},{3,1},{4,6},{5,7},{6,4},{7,5},{8,10},{9,11},{10,... | collective-permute-start | bytes 442376 | tf_op jit(solution)/shard_map/ppermute | solution.py:620
  517.7 4.1 collective-permute-start.15
  521.9 17.4 %collective-permute-start.16 = (f32[2,384]{1,0:T(2,128)S(1)}, f32[2,384]{1,0:T(2,128)S(1)}, u32[]{:S(2)}, u32[]{:S(2)}) collective-permute-start(f32[2,384]{1,0:T(2,128)S(1)} %add.104), channel_id=1, source_target_pairs={{0,2},{1,3},{2,0},{3,1},{4,6},{5,7},{6,4},{7,5},{8,10},{9,11},{10,... | collective-permute-start | bytes 9224 | tf_op jit(solution)/shard_map/ppermute | solution.py:620
  539.3 19.6 %collective-permute-start.17 = (f32[2,384]{1,0:T(2,128)S(1)}, f32[2,384]{1,0:T(2,128)S(1)}, u32[]{:S(2)}, u32[]{:S(2)}) collective-permute-start(f32[2,384]{1,0:T(2,128)S(1)} %add.105), channel_id=1, source_target_pairs={{0,4},{1,5},{2,6},{3,7},{4,0},{5,1},{6,2},{7,3},{8,12},{9,13},{10,... | collective-permute-start | bytes 9224 | tf_op jit(solution)/shard_map/ppermute | solution.py:620
  557.4 5.7 collective-permute-start.12
  589.7 6.6 collective-permute-start.18
  589.7 139.6 %all-to-all-start.5 = ((bf16[256,16,384]{2,1,0:T(8,128)(2,1)}), bf16[256,16,384]{2,1,0:T(8,128)(2,1)}, u32[]{:S(2)}, u32[]{:S(2)}) async-start(bf16[256,16,384]{2,1,0:T(8,128)(2,1)} %bitcast.64), calls=%async_computation.5 | async-start | bytes 6291456 | tf_op jit(solution)/shard_map/all_to_all | solution.py:628
  594.2 135.2 %all-gather.3.cloned.1.call-start = ((), (), s32[]{:S(2)}) async-start(), calls=%async_computation.7 | async-start | bytes 2433024 | tf_op jit(solution)/shard_map/all_gather | solution.py:739
  599.6 1.8 copy-start.1
  601.6 41.2 %collective-permute-start.19 = (bf16[1,1,18,2,64,384]{5,4,3,2,1,0:T(8,128)(2,1)S(1)}, bf16[1,1,18,2,64,384]{5,4,3,2,1,0:T(8,128)(2,1)S(1)}, u32[]{:S(2)}, u32[]{:S(2)}) collective-permute-start(bf16[1,1,18,2,64,384]{5,4,3,2,1,0:T(8,128)(2,1)S(1)} %constant_dynamic-slice_fusion), channel_id=1, source_target_pairs={{0,16},{8,24},{16,0},{24,8},{1,17},{9,25},{17,1},{25,9},{2,18},{10... | collective-permute-start | bytes 5308424 | tf_op jit(solution)/shard_map/ppermute | solution.py:620
  645.2 95.5 %copy-start = (bf16[16,2,64,384]{3,2,1,0:T(8,128)(2,1)}, bf16[16,2,64,384]{3,2,1,0:T(8,128)(2,1)S(1)}, u32[]{:S(2)}) copy-start(bf16[16,2,64,384]{3,2,1,0:T(8,128)(2,1)S(1)} %slice_bitcast_fusion.refs_3_.rest_0_) | copy-start | bytes 4718596
  645.2 35.8 %collective-permute-start.23 = (bf16[16,2,64,384]{3,2,1,0:T(8,128)(2,1)S(1)}, bf16[16,2,64,384]{3,2,1,0:T(8,128)(2,1)S(1)}, u32[]{:S(2)}, u32[]{:S(2)}) collective-permute-start(bf16[16,2,64,384]{3,2,1,0:T(8,128)(2,1)S(1)} %slice_bitcast_fusion.refs_3_.rest_0_), channel_id=1, source_target_pairs={{0,16},{8,24},{16,0},{24,8},{1,17},{9,25},{17,1},{25,9},{2,18},{10... | collective-permute-start | bytes 4718600 | tf_op jit(solution)/shard_map/ppermute | solution.py:620
  647.7 93.0 %collective-permute-start.20 = (bf16[16,2,64,384]{3,2,1,0:T(8,128)(2,1)S(1)}, bf16[16,2,64,384]{3,2,1,0:T(8,128)(2,1)}, u32[]{:S(2)}, u32[]{:S(2)}) collective-permute-start(bf16[16,2,64,384]{3,2,1,0:T(8,128)(2,1)S(1)} %slice_bitcast_fusion.refs_3_.rest_0_), channel_id=1, source_target_pairs={{0,7},{1,6},{2,5},{3,4},{4,3},{5,2},{6,1},{7,0},{8,15},{9,14},{10,... | collective-permute-start | bytes 4718600 | tf_op jit(solution)/shard_map/ppermute | solution.py:620
  649.3 91.4 %collective-permute-start.22 = (bf16[16,2,64,384]{3,2,1,0:T(8,128)(2,1)S(1)}, bf16[16,2,64,384]{3,2,1,0:T(8,128)(2,1)}, u32[]{:S(2)}, u32[]{:S(2)}) collective-permute-start(bf16[16,2,64,384]{3,2,1,0:T(8,128)(2,1)S(1)} %slice_bitcast_fusion.refs_3_.rest_0_), channel_id=1, source_target_pairs={{0,8},{8,0},{16,24},{24,16},{1,9},{9,1},{17,25},{25,17},{2,10},{10... | collective-permute-start | bytes 4718600 | tf_op jit(solution)/shard_map/ppermute | solution.py:620
  681.0 59.8 %copy-start.7 = (bf16[16,2,64,384]{3,2,1,0:T(8,128)(2,1)}, bf16[16,2,64,384]{3,2,1,0:T(8,128)(2,1)S(1)}, u32[]{:S(2)}) copy-start(bf16[16,2,64,384]{3,2,1,0:T(8,128)(2,1)S(1)} %collective-permute-done.23.refs_5_.rest_2_) | copy-start | bytes 4718596
  681.0 59.8 %collective-permute-start.24 = (bf16[16,2,64,384]{3,2,1,0:T(8,128)(2,1)S(1)}, bf16[16,2,64,384]{3,2,1,0:T(8,128)(2,1)}, u32[]{:S(2)}, u32[]{:S(2)}) collective-permute-start(bf16[16,2,64,384]{3,2,1,0:T(8,128)(2,1)S(1)} %collective-permute-done.23.refs_5_.rest_2_), channel_id=1, source_target_pairs={{0,8},{8,0},{16,24},{24,16},{1,9},{9,1},{17,25},{25,17},{2,10},{10... | collective-permute-start | bytes 4718600 | tf_op jit(solution)/shard_map/ppermute | solution.py:620
  681.0 59.7 %collective-permute-start.21 = (bf16[2,64,384]{2,1,0:T(8,128)(2,1)S(1)}, bf16[2,64,384]{2,1,0:T(8,128)(2,1)S(1)}, u32[]{:S(2)}, u32[]{:S(2)}) collective-permute-start(bf16[2,64,384]{2,1,0:T(8,128)(2,1)S(1)} %fusion.1), channel_id=1, source_target_pairs={{0,4},{1,7},{2,6},{3,5},{8,12},{9,15},{10,14},{11,13},{16,20},{17,... | collective-permute-start | bytes 294920 | tf_op jit(solution)/shard_map/ppermute | solution.py:751
  740.7 0.6 copy-start.13
  741.4 11.8 %copy-start.14 = (bf16[2,64,384]{2,1,0:T(8,128)(2,1)S(1)}, bf16[2,64,384]{2,1,0:T(8,128)(2,1)}, u32[]{:S(2)}) copy-start(bf16[2,64,384]{2,1,0:T(8,128)(2,1)} %copy-done.13) | copy-start | bytes 294916
  741.4 82.7 %all-to-all-start.6 = ((bf16[256,16,384]{2,1,0:T(8,128)(2,1)}), bf16[256,16,384]{2,1,0:T(8,128)(2,1)S(1)}, u32[]{:S(2)}, u32[]{:S(2)}) async-start(bf16[256,16,384]{2,1,0:T(8,128)(2,1)} %hold.7), calls=%async_computation.6 | async-start | bytes 6291456 | tf_op jit(solution)/shard_map/all_to_all | solution.py:628
  753.1 41.5 %copy-start.20 = (f32[2,384]{1,0:T(2,128)S(1)}, f32[2,384]{1,0:T(2,128)}, u32[]{:S(2)}) copy-start(f32[2,384]{1,0:T(2,128)} %add_multiply_fusion.rest_4_) | copy-start | bytes 9220
  753.1 42.1 %copy-start.6 = (bf16[1,1,1,1,1,768,1536]{6,5,4,3,2,1,0:T(8,128)(2,1)S(1)}, bf16[1,1,1,1,1,768,1536]{6,5,4,3,2,1,0:T(8,128)(2,1)}, u32[]{:S(2)}) copy-start(bf16[1,1,1,1,1,768,1536]{6,5,4,3,2,1,0:T(8,128)(2,1)} %all-gather.3.cloned.1.call-done) | copy-start | bytes 7077892
  756.1 38.5 %collective-permute-start.26 = (bf16[17,2,64,384]{3,2,1,0:T(8,128)(2,1)}, bf16[17,2,64,384]{3,2,1,0:T(8,128)(2,1)}, u32[]{:S(2)}, u32[]{:S(2)}) collective-permute-start(bf16[17,2,64,384]{3,2,1,0:T(8,128)(2,1)} %pad_maximum_fusion.1.rest_4_), channel_id=1, source_target_pairs={{0,16},{8,24},{16,0},{24,8},{1,17},{9,25},{17,1},{25,9},{2,18},{10... | collective-permute-start | bytes 5013512 | tf_op jit(solution)/shard_map/ppermute | solution.py:620
  757.5 41.7 %collective-permute-start.25 = (bf16[17,2,64,384]{3,2,1,0:T(8,128)(2,1)}, bf16[17,2,64,384]{3,2,1,0:T(8,128)(2,1)}, u32[]{:S(2)}, u32[]{:S(2)}) collective-permute-start(bf16[17,2,64,384]{3,2,1,0:T(8,128)(2,1)} %pad_maximum_fusion.1.rest_4_), channel_id=1, source_target_pairs={{0,8},{8,0},{16,24},{24,16},{1,9},{9,1},{17,25},{25,17},{2,10},{10... | collective-permute-start | bytes 5013512 | tf_op jit(solution)/shard_map/ppermute | solution.py:620
  794.6 4.5 collective-permute-start.27
  824.0 1.6 copy-start.2
Sparse Core Ops, SparseCore 0:
  603.3 126.0 all-gather.2
